TPU v7x, 1024 devices: a whole 8x8x8 slice. The times are simulated.
1024 devices in a mesh: emb: 64 (over z, y), bal: 8 (over x), rep: 2 (over core).
Axes of the slice: x: 8, y: 8, z: 8, core: 2. Of those that a mesh axis runs over, the one named last changes fastest.
Arguments:
- table: bfloat16 [16384, 512], P('emb'), may hold values from -4 to 4
- served_rows: int32 [64, 8, 2, 512], P('emb', 'bal', 'rep'), may hold values from 0 to 255
- w_in: bfloat16 [512, 2048], replicated, may hold values from -0.25 to 0.25
- w_out: bfloat16 [512, 512], replicated, may hold values from -0.25 to 0.25
- lookup_slots: int32 [128, 1024, 2], P(('emb', 'rep'), 'bal'), may hold values from 0 to 511, as said below
- block_users: int32 [128, 8], P(('emb', 'rep')), may hold values from 0 to 1, as said below
- out_grad: bfloat16 [128, 1024, 512], P(('emb', 'rep'), 'bal'), may hold values from -6 to 6
Outputs:
- layer_out: bfloat16 [128, 1024, 512], P(('emb', 'rep'), 'bal')
- table_grad: float32 [16384, 512], P('emb')
Inputs may be any that keep to these rules, and one draw needn't show every extreme that they name: `lookup_slots`: on one device (one group g and one b), the 2 entries of all its 128 events are distinct, each naming shard p // 8 and slot p % 8. `block_users`: never falling along a group; every user 0 to 1 of every group holds 2 to 6 blocks, and in every draw some group has a user with exactly 6 blocks.
All inputs are finite; a program needn't handle non-finite values.
Results may differ from a plain program's by a relative error of at most 0.02.
Values may be sent and summed in bfloat16 or wider, within the bound.
A program may use at most 64 MiB of HBM per device.

v0:
```python
import math

import jax
import jax.numpy as jnp
from jax import lax
from jax.sharding import PartitionSpec as P

HEADS = 4
BLK = 128


epsilon = 1e-05


def normalize(inputs):
    average = jnp.mean(inputs, axis=-1, keepdims=True)
    centered = inputs - average
    spread = jnp.sqrt(jnp.mean(centered * centered, axis=-1, keepdims=True) + epsilon)
    return (centered / spread, spread)


def normalize_back(grads, normed, spread):
    first_term = jnp.mean(grads, axis=-1, keepdims=True)
    second_term = jnp.mean(grads * normed, axis=-1, keepdims=True)
    return (grads - first_term - normed * second_term) / spread


def silu_slope(inputs):
    sigmoid_val = jax.nn.sigmoid(inputs)
    return sigmoid_val * (1.0 + inputs * (1.0 - sigmoid_val))


def per_device(table, served_rows, w_in, w_out, lookup_slots, block_users, out_grad):
    peer_count = lax.axis_size("emb")
    feat_width = table.shape[1]
    rows_dev = lookup_slots.shape[1]
    feat_count = lookup_slots.shape[2]
    head_dim = feat_width // HEADS
    inv_root = 1.0 / math.sqrt(head_dim)
    served = served_rows.reshape(peer_count, -1)
    outgoing = table[served]
    incoming = lax.all_to_all(outgoing, "emb", split_axis=0, concat_axis=0, tiled=True).reshape(
        -1, feat_width
    )
    lookup_pos = lookup_slots[0]
    events = jnp.sum(incoming[lookup_pos].astype(jnp.float32), axis=1)
    normed_in, sigma_in = normalize(events)
    pre_act = jnp.dot(normed_in.astype(jnp.bfloat16), w_in, preferred_element_type=jnp.float32)
    activations = jax.nn.silu(pre_act).astype(jnp.bfloat16)
    gate_part = activations[:, :feat_width].astype(jnp.float32)
    value_rows = activations[:, feat_width : 2 * feat_width]
    query_rows = activations[:, 2 * feat_width : 3 * feat_width]
    key_rows = activations[:, 3 * feat_width :]
    key_all, value_all = (
        lax.all_gather(key_rows, "bal", axis=0, tiled=True),
        lax.all_gather(value_rows, "bal", axis=0, tiled=True),
    )
    group_tok = key_all.shape[0]
    user_tok = jnp.repeat(block_users[0], BLK, total_repeat_length=group_tok)
    first_row = lax.axis_index("bal") * rows_dev
    query_pos = first_row + jnp.arange(rows_dev, dtype=jnp.int32)
    query_users = lax.dynamic_slice_in_dim(user_tok, first_row, rows_dev)
    key_pos = jnp.arange(group_tok, dtype=jnp.int32)
    same_user = query_users[:, None] == user_tok[None, :]
    user_length = jnp.sum(same_user.astype(jnp.float32), axis=1)
    visible = same_user & (query_pos[:, None] >= key_pos[None, :])
    query_heads = query_rows.reshape(rows_dev, HEADS, head_dim)
    key_heads = key_all.reshape(group_tok, HEADS, head_dim)
    value_heads = value_all.reshape(group_tok, HEADS, head_dim)
    scores = (
        jnp.einsum("ihd,jhd->hij", query_heads, key_heads, preferred_element_type=jnp.float32)
        * inv_root
    )
    weights = jnp.where(
        visible[None], jax.nn.silu(scores) / user_length[None, :, None], 0.0
    ).astype(jnp.bfloat16)
    attended = jnp.einsum(
        "hij,jhd->ihd", weights, value_heads, preferred_element_type=jnp.float32
    ).reshape(rows_dev, feat_width)
    normed_att, sigma_att = normalize(attended)
    mixed = (normed_att * gate_part).astype(jnp.bfloat16)
    layer_out = (events + jnp.dot(mixed, w_out, preferred_element_type=jnp.float32)).astype(
        jnp.bfloat16
    )
    grad_rows = out_grad[0]
    d_mixed = jnp.dot(grad_rows, w_out.T, preferred_element_type=jnp.float32)
    d_gate = d_mixed * normed_att
    d_att = normalize_back(d_mixed * gate_part, normed_att, sigma_att).astype(jnp.bfloat16)
    d_heads = d_att.reshape(rows_dev, HEADS, head_dim)
    d_weights = jnp.einsum("ihd,jhd->hij", d_heads, value_heads, preferred_element_type=jnp.float32)
    d_scores = jnp.where(
        visible[None], d_weights * silu_slope(scores) / user_length[None, :, None], 0.0
    ).astype(jnp.bfloat16)
    d_queries = (
        jnp.einsum("hij,jhd->ihd", d_scores, key_heads, preferred_element_type=jnp.float32).reshape(
            rows_dev, feat_width
        )
        * inv_root
    )
    row_count = rows_dev * lax.axis_size("bal")
    weight_cols = lax.slice_in_dim(weights, 0, row_count, axis=2)
    score_cols = lax.slice_in_dim(d_scores, 0, row_count, axis=2)
    value_term = jnp.einsum(
        "hij,ihd->jhd", weight_cols, d_heads, preferred_element_type=jnp.float32
    ).reshape(row_count, feat_width)
    key_term = (
        jnp.einsum(
            "hij,ihd->jhd", score_cols, query_heads, preferred_element_type=jnp.float32
        ).reshape(row_count, feat_width)
        * inv_root
    )
    key_grads = lax.psum_scatter(
        jnp.concatenate([key_term, value_term], axis=1).astype(jnp.bfloat16),
        "bal",
        scatter_dimension=0,
        tiled=True,
    ).astype(jnp.float32)
    d_keys = key_grads[:, :feat_width]
    d_values = key_grads[:, feat_width:]
    d_acts = jnp.concatenate([d_gate, d_values, d_queries, d_keys], axis=1)
    d_pre = (d_acts * silu_slope(pre_act)).astype(jnp.bfloat16)
    d_normed = jnp.dot(d_pre, w_in.T, preferred_element_type=jnp.float32)
    d_events = (
        grad_rows.astype(jnp.float32) + normalize_back(d_normed, normed_in, sigma_in)
    ).astype(jnp.bfloat16)
    spread_rows = jnp.broadcast_to(
        d_events[:, None, :], (rows_dev, feat_count, feat_width)
    ).reshape(-1, feat_width)
    send_back = (
        jnp.zeros((incoming.shape[0], feat_width), jnp.bfloat16)
        .at[lookup_pos.reshape(-1)]
        .set(spread_rows)
    )
    returned = lax.all_to_all(
        send_back.reshape(peer_count, -1, feat_width),
        "emb",
        split_axis=0,
        concat_axis=0,
        tiled=True,
    )
    local_grad = (
        jnp.zeros((table.shape[0], feat_width), jnp.float32)
        .at[served.reshape(-1)]
        .add(returned.reshape(-1, feat_width).astype(jnp.float32))
    )
    table_grad = lax.psum(local_grad.astype(jnp.bfloat16), ("bal", "rep")).astype(jnp.float32)
    return (layer_out[None], table_grad)


def solution(mesh):
    placed = (
        P("emb", None),
        P("emb", "bal", "rep", None),
        P(),
        P(),
        P(("emb", "rep"), "bal", None),
        P(("emb", "rep"), None),
        P(("emb", "rep"), "bal", None),
    )
    return jax.shard_map(
        per_device,
        mesh=mesh,
        in_specs=placed,
        out_specs=(P(("emb", "rep"), "bal", None), P("emb", None)),
        check_vma=False,
    )
```

profile of v0, /device:TPU:1, one launch (start us, length us, event | category | flops | bytes accessed | tf_op | source)
XLA Modules:
  0.0 371.8 jit_solution(2858648254455878645)
XLA Ops:
  7.7 1.5 reduce.14
  9.4 3.6 gather_fusion
  13.0 24.0 %all-to-all-start = ((bf16[64,8,512]{2,1,0:T(8,128)(2,1)}), bf16[64,8,512]{2,1,0:T(8,128)(2,1)S(1)}, u32[]{:S(2)}, u32[]{:S(2)}) async-start(bf16[64,8,512]{2,1,0:T(8,128)(2,1)} %bitcast), calls=%async_computation | async-start | bytes 1048576 | tf_op jit(solution)/shard_map/all_to_all | solution.py:42
  37.3 16.8 %all-to-all-done = bf16[64,8,512]{2,1,0:T(8,128)(2,1)S(1)} async-done(((bf16[64,8,512]{2,1,0:T(8,128)(2,1)}), bf16[64,8,512]{2,1,0:T(8,128)(2,1)S(1)}, u32[]{:S(2)}, u32[]{:S(2)}) %all-to-all-start) | async-done | bytes 524320 | tf_op jit(solution)/shard_map/all_to_all | solution.py:42
  54.1 1.2 gather_fusion.1
  56.9 1.5 multiply_convert_fusion.1
  61.6 4.4 %compare_select_fusion.2 = s32[1024,1]{0,1:T(1,128)S(1)} fusion(s32[]{:T(128)} %bitcast.8, s32[]{:T(128)} %bitcast.9, s32[]{:T(128)} %bitcast.10, s32[]{:T(128)} %bitcast.11, s32[]{:T(128)} %bitcast.12, s32[]{:T(128)} %bitcast.14, s32[]{:T(128)} %bitcast.13, s32[1024,1]{0,1:T(1,128)S(1)} %bitcast.109, s32[1024,1]{0,1:T(1,128)S(1)} %bitcast.107), kind=kLoop, calls=%fused_computation.57 | loop fusion | flops 14336 | bytes 12316 | tf_op jit(solution)/shard_map/jit(_take)/gather | solution.py:59
  67.3 27.2 %all-gather.5.cloned.1.call-done = bf16[1024,512]{1,0:T(8,128)(2,1)} async-done(((bf16[128,512]{1,0:T(8,128)(2,1)}), bf16[1024,512]{1,0:T(8,128)(2,1)}) %all-gather.5.cloned.1.call-update) | async-done | bytes 1048592 | tf_op jit(solution)/shard_map/all_gather | solution.py:55
  94.5 2.3 copy.40
  96.8 3.5 select_convert_fusion.1
  100.3 40.5 %all-gather.3.cloned.1.call-done = bf16[1024,512]{1,0:T(8,128)(2,1)} async-done(((bf16[128,512]{1,0:T(8,128)(2,1)}), bf16[1024,512]{1,0:T(8,128)(2,1)}) %all-gather.3.cloned.1.call-update) | async-done | bytes 1048592 | tf_op jit(solution)/shard_map/all_gather | solution.py:56
  140.8 1.8 fusion.36
  144.0 1.6 fusion.26
  145.6 1.9 fusion.31
  147.6 1.4 convolution_convert_fusion
  149.1 2.8 select_convert_fusion
  152.9 1.4 multiply_convert_fusion
  154.3 1.3 copy.37
  155.7 2.4 copy.36
  158.0 2.9 pad_maximum_fusion
  162.2 2.4 convolution_multiply_fusion
  164.5 1.1 copy.38
  165.6 43.2 %reduce-scatter.2.cloned.1.call-done = bf16[128,1024]{1,0:T(8,128)(2,1)} async-done(((bf16[1024,1024]{1,0:T(8,128)(2,1)}), bf16[128,1024]{1,0:T(8,128)(2,1)}) %reduce-scatter.2.cloned.1.call-update) | async-done | bytes 262160 | tf_op jit(solution)/shard_map/reduce_scatter | solution.py:112
  208.9 1.0 fusion.34
  209.9 2.3 fusion.32
  212.6 2.3 scatter_custom_fusion
  215.0 13.4 %all-to-all-start.1 = ((bf16[64,8,512]{2,1,0:T(8,128)(2,1)}), bf16[64,8,512]{2,1,0:T(8,128)(2,1)S(1)}, u32[]{:S(2)}, u32[]{:S(2)}) async-start(bf16[64,8,512]{2,1,0:T(8,128)(2,1)} %bitcast.29), calls=%async_computation.2 | async-start | bytes 1048576 | tf_op jit(solution)/shard_map/all_to_all | solution.py:134
  228.7 14.2 %all-to-all-done.1 = bf16[64,8,512]{2,1,0:T(8,128)(2,1)S(1)} async-done(((bf16[64,8,512]{2,1,0:T(8,128)(2,1)}), bf16[64,8,512]{2,1,0:T(8,128)(2,1)S(1)}, u32[]{:S(2)}, u32[]{:S(2)}) %all-to-all-start.1) | async-done | bytes 524320 | tf_op jit(solution)/shard_map/all_to_all | solution.py:134
  242.9 3.8 %scatter_custom_fusion.1 = f32[256,512]{1,0:T(8,128)S(1)} fusion(s32[512]{0:T(512)S(1)} %bitcast.111, bf16[64,8,512]{2,1,0:T(8,128)(2,1)S(1)} %all-to-all-done.1, f32[]{:T(128)} %constant.116.clone.1), kind=kCustom, calls=%fused_computation.19 | custom fusion | flops 524288 | bytes 1048580 | tf_op jit(solution)/shard_map/scatter-add | solution.py:144
  247.4 2.1 fusion.1
  249.6 113.9 %all-reduce.2.cloned.1.call-done = bf16[256,512]{1,0:T(8,128)(2,1)} async-done(((bf16[256,512]{1,0:T(8,128)(2,1)}), bf16[256,512]{1,0:T(8,128)(2,1)}) %all-reduce.2.cloned.1.call-update) | async-done | bytes 262160 | tf_op jit(solution)/shard_map/psum | solution.py:146
  363.5 1.8 convert_element_type.72
  (86 shorter events, 12.1 us)
Async XLA Ops:
  7.2 49.7 %copy-start = (bf16[512,2048]{1,0:T(8,128)(2,1)S(1)}, bf16[512,2048]{1,0:T(8,128)(2,1)}, u32[]{:S(2)}) copy-start(bf16[512,2048]{1,0:T(8,128)(2,1)} %param.11) | copy-start | bytes 6291460
  9.4 27.7 %copy-start.14 = (s32[1,128,2]{1,2,0:T(2,128)S(1)}, s32[1,128,2]{1,2,0:T(2,128)}, u32[]{:S(2)}) copy-start(s32[1,128,2]{1,2,0:T(2,128)} %param.13) | copy-start | bytes 3076
  13.0 41.1 %all-to-all-start = ((bf16[64,8,512]{2,1,0:T(8,128)(2,1)}), bf16[64,8,512]{2,1,0:T(8,128)(2,1)S(1)}, u32[]{:S(2)}, u32[]{:S(2)}) async-start(bf16[64,8,512]{2,1,0:T(8,128)(2,1)} %bitcast), calls=%async_computation | async-start | bytes 1048576 | tf_op jit(solution)/shard_map/all_to_all | solution.py:42
  37.0 57.5 %all-gather.5.cloned.1.call-start = ((), (), s32[]{:S(2)}) async-start(), calls=%async_computation.4 | async-start | bytes 1179648 | tf_op jit(solution)/shard_map/all_gather | solution.py:55
  56.6 1.7 copy-start.5
  56.9 4.1 %copy-start.12 = (s32[1,8]{1,0:T(1,128)S(1)}, s32[1,8]{1,0:T(1,128)}, u32[]{:S(2)}) copy-start(s32[1,8]{1,0:T(1,128)} %param.14) | copy-start | bytes 100
  58.4 0.8 copy-start.8
  59.9 80.9 %all-gather.3.cloned.1.call-start = ((), (), s32[]{:S(2)}) async-start(), calls=%async_computation.3 | async-start | bytes 1179648 | tf_op jit(solution)/shard_map/all_gather | solution.py:56
  60.7 148.2 %reduce-scatter.2.cloned.1.call-start = ((), (), s32[]{:S(2)}) async-start(), calls=%async_computation.5 | async-start | bytes 2359296 | tf_op jit(solution)/shard_map/reduce_scatter | solution.py:112
  66.9 33.4 %copy-start.16 = (f32[128]{0:T(128)}, f32[128]{0:T(128)S(1)}, u32[]{:S(2)}) copy-start(f32[128]{0:T(128)S(1)} %fusion.10) | copy-start | bytes 1540
  67.1 33.2 %copy-start.9 = (pred[128,1024]{1,0:T(8,128)(4,1)}, pred[128,1024]{1,0:T(8,128)(4,1)S(1)}, u32[]{:S(2)}) copy-start(pred[128,1024]{1,0:T(8,128)(4,1)S(1)} %compare_and_fusion) | copy-start | bytes 393220
  147.6 1.5 copy-start.7
  147.6 1.5 copy-start.10
  151.9 1.0 copy-start.2
  152.9 1.4 copy-start.3
  155.7 2.4 copy-start.4
  160.9 1.2 copy-start.1
  161.0 48.9 %copy-start.6 = (f32[128,512]{1,0:T(8,128)S(1)}, f32[128,512]{1,0:T(8,128)}, u32[]{:S(2)}) copy-start(f32[128,512]{1,0:T(8,128)} %copy-done.5) | copy-start | bytes 786436
  209.9 2.3 copy-start.11
  212.2 16.5 %copy-start.13 = (s32[1,1,1,512]{3,2,1,0:T(1,128)S(1)}, s32[1,1,1,512]{3,2,1,0:T(1,128)}, u32[]{:S(2)}) copy-start(s32[1,1,1,512]{3,2,1,0:T(1,128)} %param.10) | copy-start | bytes 6148
  212.5 34.9 %copy-start.15 = (f32[128]{0:T(128)S(1)}, f32[128]{0:T(128)}, u32[]{:S(2)}) copy-start(f32[128]{0:T(128)} %add_sqrt_fusion) | copy-start | bytes 1540
  215.0 27.9 %all-to-all-start.1 = ((bf16[64,8,512]{2,1,0:T(8,128)(2,1)}), bf16[64,8,512]{2,1,0:T(8,128)(2,1)S(1)}, u32[]{:S(2)}, u32[]{:S(2)}) async-start(bf16[64,8,512]{2,1,0:T(8,128)(2,1)} %bitcast.29), calls=%async_computation.2 | async-start | bytes 1048576 | tf_op jit(solution)/shard_map/all_to_all | solution.py:134
  228.4 135.1 %all-reduce.2.cloned.1.call-start = ((), (), s32[]{:S(2)}) async-start(), calls=%async_computation.6 | async-start | bytes 524288 | tf_op jit(solution)/shard_map/psum | solution.py:146
Sparse Core Ops, SparseCore 0:
  60.0 34.3 all-gather.4
  97.7 43.0 all-gather.2
  161.1 47.7 reduce-scatter.1
  247.5 115.9 all-reduce.1
where the time goes:
time: 373 us; the launch traced here: 372 us
  waiting for transfers between devices  257 us (69%)
  starting transfers between devices  38 us (10%)
  local copies, waits for them, and re-layouts  22.4 us (6%)
  matrix products  20.9 us (6%)
  other arithmetic  19.8 us (5%)
  between operations  14.2 us (4%)
    psum x1, waiting for transfers between devices, per_device(): lax.psum(local_grad.astype(jnp.bfloat16), ('bal', 'rep'))  114 us
    reduce_scatter x1, waiting for transfers between devices, per_device(): lax.psum_scatter(jnp.concatenate([key_term, value_term], axis=1).astype(j...  43.2 us
    all_gather x1, waiting for transfers between devices, per_device(): lax.all_gather(value_rows, 'bal', axis=0, tiled=True)  40.5 us
    all_gather x1, waiting for transfers between devices, per_device(): lax.all_gather(key_rows, 'bal', axis=0, tiled=True)  27.2 us
    all_to_all x1, starting transfers between devices, per_device(): lax.all_to_all(outgoing, 'emb', split_axis=0, concat_axis=0, tiled=True)  24 us
    all_to_all x1, waiting for transfers between devices, per_device(): lax.all_to_all(outgoing, 'emb', split_axis=0, concat_axis=0, tiled=True)  16.8 us
    all_to_all x1, waiting for transfers between devices, per_device(): lax.all_to_all(send_back.reshape(peer_count, -1, feat_width), 'emb', spli...  14.2 us
    all_to_all x1, starting transfers between devices, per_device(): lax.all_to_all(send_back.reshape(peer_count, -1, feat_width), 'emb', spli...  13.4 us
  transfers between devices with their start and end apart: 6, of which 6 were waited for; matrix products, arithmetic and copies ran while one was open for 5% of the time, Pallas kernels for 0%

commit v1 on v0

v1 whole, which is shorter than its diff:
```python
import functools
import math

import jax
import jax.numpy as jnp
from jax import lax
from jax.experimental import pallas as pl
from jax.experimental.pallas import tpu as pltpu
from jax.sharding import PartitionSpec as P

HEADS = 4
EPS = 1e-05
MESH = pl.DeviceIdType.MESH
F32 = jnp.float32
BF16 = jnp.bfloat16


def dot(a, b):
    return jnp.dot(a, b, preferred_element_type=F32)


def dot_nt(a, b):
    return lax.dot_general(a, b, (((1,), (1,)), ((), ())), preferred_element_type=F32)


def dot_tn(a, b):
    return lax.dot_general(a, b, (((0,), (0,)), ((), ())), preferred_element_type=F32)


def sigmoid(v):
    return 0.5 * jnp.tanh(0.5 * v) + 0.5


def silu(v):
    return v * sigmoid(v)


def silu_and_slope(v):
    s = sigmoid(v)
    y = v * s
    return y, s + y * (1.0 - s)


def row_mean(v):
    return jnp.mean(v, axis=-1, keepdims=True)


def layer_kernel(
    sizes,
    table_ref, idx_ref, lookup_ref, users_ref, w_in_hbm, w_out_hbm, grad_hbm,
    layer_ref, tgrad_ref,
    w_in, w_out, grad, zout, zin, zback, zret, onehot, look,
    events, normed, inv_in, act, slope, nrm, datt, kv, qall,
    wt, gt, gq, att, dq, dk, dv, gsend, rsbuf, agbuf,
    load_sem, a1_send, a1_recv, x1_send, x1_recv, x2_send, x2_recv,
    a2_send, a2_recv, rs_send, rs_recv, ag_send, ag_recv,
):
    n_emb, n_bal, n_rep = sizes
    tok, width = grad.shape
    half = width // 2
    slab = zout.shape[0] // n_emb
    cap = slab // 2
    trows = table_ref.shape[0]
    hd = width // HEADS
    inv_root = 1.0 / math.sqrt(hd)
    e = lax.axis_index("emb")
    b = lax.axis_index("bal")
    rep = lax.axis_index("rep")
    n_red = n_bal * n_rep
    mine = b * n_rep + rep
    part = gsend.shape[0] // n_red

    def red_peer(k):
        c = lax.rem(mine + k, n_red)
        return c, {"bal": lax.div(c, n_rep), "rep": lax.rem(c, n_rep)}

    loads = [
        pltpu.make_async_copy(src, dst, load_sem.at[i])
        for i, (src, dst) in enumerate(((w_in_hbm, w_in), (w_out_hbm, w_out), (grad_hbm, grad)))
    ]
    for load in loads:
        load.start()

    barrier = pltpu.get_barrier_semaphore()

    @pl.loop(1, n_emb)
    def _(k):
        pl.semaphore_signal(
            barrier, inc=1, device_id={"emb": lax.rem(e + k, n_emb)}, device_id_type=MESH
        )

    @pl.loop(1, n_red)
    def _(k):
        _, where = red_peer(k)
        pl.semaphore_signal(barrier, inc=1, device_id=where, device_id_type=MESH)

    rows_of = lax.broadcasted_iota(jnp.int32, onehot.shape, 0)
    onehot[...] = jnp.where(rows_of == idx_ref[...], 1.0, 0.0).astype(BF16)
    stacked = jnp.concatenate([table_ref[:, :half], table_ref[:, half:]], axis=0)
    zout[...] = dot_tn(onehot[...], stacked).astype(BF16)

    pl.semaphore_wait(barrier, n_emb - 1 + n_red - 1)

    def exchange(src, dst, send, recv):
        own = pl.ds(pl.multiple_of(e * slab, slab), slab)

        @pl.loop(1, n_emb)
        def _(k):
            to = lax.rem(e + k, n_emb)
            pltpu.make_async_remote_copy(
                src_ref=src.at[pl.ds(pl.multiple_of(to * slab, slab), slab)],
                dst_ref=dst.at[own],
                send_sem=send,
                recv_sem=recv,
                device_id={"emb": to},
                device_id_type=MESH,
            ).start()

        dst[own, :] = src[own, :]
        many = pl.ds(0, (n_emb - 1) * slab)
        return pltpu.make_async_remote_copy(
            src_ref=src.at[many],
            dst_ref=dst.at[many],
            send_sem=send,
            recv_sem=recv,
            device_id={"emb": lax.rem(e + 1, n_emb)},
            device_id_type=MESH,
        )

    first = exchange(zout, zin, a1_send, a1_recv)

    p = lookup_ref[...]
    slot = lax.shift_right_logical(p, int(math.log2(cap))) * slab + (p & (cap - 1))
    cols_of = lax.broadcasted_iota(jnp.int32, (tok, zout.shape[0]), 1)
    for h in range(2):
        q = slot + h * cap
        hit = (cols_of == q[:, 0:1]) | (cols_of == q[:, 1:2])
        look[h * tok : (h + 1) * tok, :] = jnp.where(hit, 1.0, 0.0).astype(BF16)

    my_user = users_ref[0, b]
    count = jnp.int32(0)
    for k in range(n_bal):
        count = count + jnp.where(users_ref[0, k] == my_user, 1, 0)
    inv_len = jnp.float32(0.0)
    for k in range(1, n_bal + 1):
        inv_len = jnp.where(count == k, jnp.float32(1.0 / (k * tok)), inv_len)

    for load in loads:
        load.wait()
    d_mixed = dot_nt(grad[...], w_out[...])

    first.wait_recv()
    two = dot(look[...], zin[...])
    events[...] = jnp.concatenate([two[:tok], two[tok:]], axis=1)
    ev = events[...]
    centered = ev - row_mean(ev)
    inv = lax.rsqrt(row_mean(centered * centered) + EPS)
    inv_in[...] = jnp.broadcast_to(inv, inv_in.shape)
    normed[...] = centered * inv
    nrm[0] = normed[...].astype(BF16)

    rows = tok // 2
    steps = n_bal // 2
    right = lax.rem(b + 1, n_bal)
    left = lax.rem(b + n_bal - 1, n_bal)

    def hop(buf, send, recv, way, step, c):
        if way == 0:
            src, dst, to = lax.rem(n_bal - step, n_bal), n_bal - 1 - step, right
        else:
            src, dst, to = step, step + 1, left
        piece = pl.ds(c * rows, rows)
        return pltpu.make_async_remote_copy(
            src_ref=buf.at[src, piece],
            dst_ref=buf.at[dst, piece],
            send_sem=send.at[way, step, c],
            recv_sem=recv.at[way, step, c],
            device_id={"bal": to},
            device_id_type=MESH,
        )

    lanes = [(way, c) for c in range(2) for way in range(2)]

    def ring_start(buf, send, recv):
        for way, c in lanes:
            if steps > 1 or way == c:
                hop(buf, send, recv, way, 0, c).start()

    def ring_rest(buf, send, recv, on_block):
        @pl.loop(0, steps)
        def _(step):
            for way, c in lanes:
                last = steps - 1 if way == c else steps - 2

                @pl.when(step <= last)
                def _():
                    hop(buf, send, recv, way, step, c).wait_recv()

                @pl.when(step + 1 <= last)
                def _():
                    hop(buf, send, recv, way, step + 1, c).start()

            @pl.loop(0, 2)
            def _(k):
                @pl.when((k == 0) | (step < steps - 1))
                def _():
                    on_block(jnp.where(k == 0, n_bal - 1 - step, step + 1))

    def ring_drain(buf, send, recv):
        @pl.loop(0, steps)
        def _(step):
            for way, c in lanes:
                last = steps - 1 if way == c else steps - 2

                @pl.when(step <= last)
                def _():
                    hop(buf, send, recv, way, step, c).wait_send()

    ring_start(nrm, x1_send, x1_recv)

    for k in (1, 2, 3, 0):
        cols = slice(k * width, (k + 1) * width)
        a, s = silu_and_slope(dot(nrm[0], w_in[:, cols]))
        act[:, cols] = a.astype(BF16)
        slope[:, cols] = s
    v_at, q_at, k_at = width, 2 * width, 3 * width

    def head(h, base=0):
        return slice(base + h * hd, base + (h + 1) * hd)

    tri_row = lax.broadcasted_iota(jnp.int32, (tok, tok), 0)
    tri_col = lax.broadcasted_iota(jnp.int32, (tok, tok), 1)
    for h in range(HEADS):
        q, k, v = act[:, head(h, q_at)], act[:, head(h, k_at)], act[:, head(h, v_at)]
        y, g = silu_and_slope(dot_nt(q, k) * inv_root)
        keep = tri_row >= tri_col
        att[:, head(h)] = dot(jnp.where(keep, y * inv_len, 0.0).astype(BF16), v)
        gq[0, h] = jnp.where(keep, g * inv_len, 0.0)
        y, g = silu_and_slope(dot_nt(k, q) * inv_root)
        keep = tri_row <= tri_col
        wt[0, h] = jnp.where(keep, y * inv_len, 0.0).astype(BF16)
        gt[0, h] = jnp.where(keep, g * inv_len, 0.0)

    def seen(j):
        return jnp.where(users_ref[0, j] == my_user, inv_len, jnp.float32(0.0))

    def forward_block(r):
        j = lax.rem(b + r, n_bal)
        f = seen(j)

        @pl.when(j < b)
        def _():
            x = nrm[r]
            kv[r, :, :width] = silu(dot(x, w_in[:, v_at : v_at + width])).astype(BF16)
            kv[r, :, width:] = silu(dot(x, w_in[:, k_at : k_at + width])).astype(BF16)
            for h in range(HEADS):
                k = kv[r, :, head(h, width)]
                y, g = silu_and_slope(dot_nt(act[:, head(h, q_at)], k) * inv_root)
                gq[r, h] = g * f
                att[:, head(h)] += dot((y * f).astype(BF16), kv[r, :, head(h)])

        @pl.when(j > b)
        def _():
            qall[r] = silu(dot(nrm[r], w_in[:, q_at : q_at + width])).astype(BF16)
            for h in range(HEADS):
                y, g = silu_and_slope(
                    dot_nt(act[:, head(h, k_at)], qall[r, :, head(h)]) * inv_root
                )
                gt[r, h] = g * f
                wt[r, h] = (y * f).astype(BF16)

    ring_rest(nrm, x1_send, x1_recv, forward_block)

    at = att[...]
    centered = at - row_mean(at)
    inv_att = lax.rsqrt(row_mean(centered * centered) + EPS)
    normed_att = centered * inv_att
    gate = act[:, :width].astype(F32)
    d_gated = d_mixed * gate
    d_att = (
        (d_gated - row_mean(d_gated) - normed_att * row_mean(d_gated * normed_att)) * inv_att
    ).astype(BF16)
    datt[0] = d_att
    ring_start(datt, x2_send, x2_recv)

    mixed = (normed_att * gate).astype(BF16)
    layer_ref[...] = (events[...] + dot(mixed, w_out[...])).astype(BF16)
    d_pre = (d_mixed * normed_att * slope[:, :width]).astype(BF16)
    gate_part = dot_nt(d_pre, w_in[:, :width])
    for h in range(HEADS):
        q, k, v = act[:, head(h, q_at)], act[:, head(h, k_at)], act[:, head(h, v_at)]
        d = datt[0, :, head(h)]
        ds = (dot_nt(d, v) * gq[0, h]).astype(BF16)
        dq[:, head(h)] = dot(ds, k)
        dv[:, head(h)] = dot(wt[0, h], d)
        dst = (dot_nt(v, d) * gt[0, h]).astype(BF16)
        dk[:, head(h)] = dot(dst, q)

    def backward_block(r):
        j = lax.rem(b + r, n_bal)

        @pl.when(j < b)
        def _():
            for h in range(HEADS):
                ds = (dot_nt(datt[0, :, head(h)], kv[r, :, head(h)]) * gq[r, h]).astype(BF16)
                dq[:, head(h)] += dot(ds, kv[r, :, head(h, width)])

        @pl.when(j > b)
        def _():
            for h in range(HEADS):
                d = datt[r, :, head(h)]
                dv[:, head(h)] += dot(wt[r, h], d)
                dst = (dot_nt(act[:, head(h, v_at)], d) * gt[r, h]).astype(BF16)
                dk[:, head(h)] += dot(dst, qall[r, :, head(h)])

    ring_rest(datt, x2_send, x2_recv, backward_block)

    d_normed = gate_part
    for base, acc, scale in ((v_at, dv, 1.0), (q_at, dq, inv_root), (k_at, dk, inv_root)):
        d_pre = (acc[...] * scale * slope[:, base : base + width]).astype(BF16)
        d_normed = d_normed + dot_nt(d_pre, w_in[:, base : base + width])
    nr = normed[...]
    d_events = (
        grad[...].astype(F32)
        + (d_normed - row_mean(d_normed) - nr * row_mean(d_normed * nr)) * inv_in[:, 0:1]
    ).astype(BF16)

    zback[...] = dot_tn(
        look[...], jnp.concatenate([d_events[:, :half], d_events[:, half:]], axis=0)
    ).astype(BF16)
    second = exchange(zback, zret, a2_send, a2_recv)
    first.wait_send()
    ring_drain(nrm, x1_send, x1_recv)
    ring_drain(datt, x2_send, x2_recv)
    second.wait_recv()
    gsend[...] = dot(onehot[...], zret[...]).astype(BF16)

    @pl.loop(1, n_red)
    def _(k):
        c, where = red_peer(k)
        pltpu.make_async_remote_copy(
            src_ref=gsend.at[pl.ds(pl.multiple_of(c * part, part), part)],
            dst_ref=rsbuf.at[pl.ds(pl.multiple_of(mine * part, part), part)],
            send_sem=rs_send,
            recv_sem=rs_recv,
            device_id=where,
            device_id_type=MESH,
        ).start()

    mine_at = pl.ds(pl.multiple_of(mine * part, part), part)
    rsbuf[mine_at, :] = gsend[mine_at, :]
    others = pl.ds(0, (n_red - 1) * part)
    _, some = red_peer(1)
    reduced = pltpu.make_async_remote_copy(
        src_ref=gsend.at[others], dst_ref=rsbuf.at[others],
        send_sem=rs_send, recv_sem=rs_recv, device_id=some, device_id_type=MESH,
    )
    second.wait_send()
    reduced.wait_recv()
    total = rsbuf[0:part, :].astype(F32)
    for k in range(1, n_red):
        total = total + rsbuf[k * part : (k + 1) * part, :].astype(F32)
    agbuf[mine_at, :] = total.astype(BF16)

    @pl.loop(1, n_red)
    def _(k):
        _, where = red_peer(k)
        pltpu.make_async_remote_copy(
            src_ref=agbuf.at[mine_at],
            dst_ref=agbuf.at[mine_at],
            send_sem=ag_send,
            recv_sem=ag_recv,
            device_id=where,
            device_id_type=MESH,
        ).start()

    gathered = pltpu.make_async_remote_copy(
        src_ref=agbuf.at[others], dst_ref=agbuf.at[others],
        send_sem=ag_send, recv_sem=ag_recv, device_id=some, device_id_type=MESH,
    )
    reduced.wait_send()
    gathered.wait_recv()
    tgrad_ref[:, :half] = agbuf[:trows, :].astype(F32)
    tgrad_ref[:, half:] = agbuf[trows:, :].astype(F32)
    gathered.wait_send()


def per_device(table, served_rows, w_in, w_out, lookup_slots, block_users, out_grad):
    n_emb, n_bal, n_rep = (lax.axis_size(a) for a in ("emb", "bal", "rep"))
    trows, width = table.shape
    tok = lookup_slots.shape[1]
    half = width // 2
    steps = n_bal // 2
    slots = 2 * served_rows.shape[-1]
    served = served_rows.reshape(n_emb, 1, -1)
    idx = jnp.concatenate([served, served + trows], axis=1).reshape(1, slots)
    hd = width // HEADS
    vmem = pl.BlockSpec(memory_space=pltpu.VMEM)
    hbm = pl.BlockSpec(memory_space=pl.ANY)
    dma = pltpu.SemaphoreType.DMA
    n_red = n_bal * n_rep
    layer_out, table_grad = pl.pallas_call(
        functools.partial(layer_kernel, (n_emb, n_bal, n_rep)),
        out_shape=(
            jax.ShapeDtypeStruct((tok, width), BF16),
            jax.ShapeDtypeStruct((trows, width), F32),
        ),
        in_specs=[vmem, vmem, vmem, pl.BlockSpec(memory_space=pltpu.SMEM), hbm, hbm, hbm],
        out_specs=(vmem, vmem),
        scratch_shapes=[
            pltpu.VMEM((width, 4 * width), BF16),
            pltpu.VMEM((width, width), BF16),
            pltpu.VMEM((tok, width), BF16),
            pltpu.VMEM((slots, half), BF16),
            pltpu.VMEM((slots, half), BF16),
            pltpu.VMEM((slots, half), BF16),
            pltpu.VMEM((slots, half), BF16),
            pltpu.VMEM((2 * trows, slots), BF16),
            pltpu.VMEM((2 * tok, slots), BF16),
            pltpu.VMEM((tok, width), F32),
            pltpu.VMEM((tok, width), F32),
            pltpu.VMEM((tok, 128), F32),
            pltpu.VMEM((tok, 4 * width), BF16),
            pltpu.VMEM((tok, 4 * width), F32),
            pltpu.VMEM((n_bal, tok, width), BF16),
            pltpu.VMEM((n_bal, tok, width), BF16),
            pltpu.VMEM((n_bal, tok, 2 * width), BF16),
            pltpu.VMEM((n_bal, tok, width), BF16),
            pltpu.VMEM((n_bal, HEADS, tok, tok), BF16),
            pltpu.VMEM((n_bal, HEADS, tok, tok), F32),
            pltpu.VMEM((n_bal, HEADS, tok, tok), F32),
            pltpu.VMEM((tok, width), F32),
            pltpu.VMEM((tok, width), F32),
            pltpu.VMEM((tok, width), F32),
            pltpu.VMEM((tok, width), F32),
            pltpu.VMEM((2 * trows, half), BF16),
            pltpu.VMEM((2 * trows, half), BF16),
            pltpu.VMEM((2 * trows, half), BF16),
            dma((3,)),
            dma, dma,
            dma((2, steps, 2)), dma((2, steps, 2)),
            dma((2, steps, 2)), dma((2, steps, 2)),
            dma, dma, dma, dma, dma, dma,
        ],
        compiler_params=pltpu.CompilerParams(
            collective_id=0, has_side_effects=True, vmem_limit_bytes=48 * 1024 * 1024
        ),
    )(table, idx, lookup_slots[0], block_users, w_in, w_out, out_grad[0])
    return layer_out[None], table_grad


def solution(mesh):
    placed = (
        P("emb", None),
        P("emb", "bal", "rep", None),
        P(),
        P(),
        P(("emb", "rep"), "bal", None),
        P(("emb", "rep"), None),
        P(("emb", "rep"), "bal", None),
    )
    return jax.shard_map(
        per_device,
        mesh=mesh,
        in_specs=placed,
        out_specs=(P(("emb", "rep"), "bal", None), P("emb", None)),
        check_vma=False,
    )
```

time: 373 us -> 116 us (0.31)
  waiting for transfers between devices: 257 us -> 0 us
  Pallas kernels: 0 us -> 106 us
  starting transfers between devices: 38 us -> 0 us
  matrix products: 20.9 us -> 0 us
  other arithmetic: 19.8 us -> 1.36 us
  local copies, waits for them, and re-layouts: 22.4 us -> 8.17 us
  between operations: 14.2 us -> 0.68 us
    psum x1 -> x0, waiting for transfers between devices: 114 us -> none  [per_device(): lax.psum(local_grad.astype(jnp.bfloat16), ('bal', 'rep'))]
    pallas_call x0 -> x1, Pallas kernels: none -> 106 us  [per_device(): pl.pallas_call(functools.partial(layer_kernel, (n_emb, n_bal, n_rep)), ou...]
    all_gather x2 -> x0, waiting for transfers between devices: 67.7 us -> none  [the longest x1 40.5 us: per_device(): lax.all_gather(value_rows, 'bal', axis=0, tiled=True)]
    reduce_scatter x1 -> x0, waiting for transfers between devices: 43.2 us -> none  [per_device(): lax.psum_scatter(jnp.concatenate([key_term, value_term], axis=1).astype(j...]
    all_to_all x2 -> x0, starting transfers between devices: 37.4 us -> none  [the longest x1 24 us: per_device(): lax.all_to_all(outgoing, 'emb', split_axis=0, concat_axis=0, tiled=True)]
    all_to_all x2 -> x0, waiting for transfers between devices: 31 us -> none  [the longest x1 16.8 us: per_device(): lax.all_to_all(outgoing, 'emb', split_axis=0, concat_axis=0, tiled=True)]
    dot_general x10 -> x0, matrix products: 20.9 us -> none  [the longest x1 3.53 us: per_device(): jnp.einsum('ihd,jhd->hij', query_heads, key_heads, preferred_element_type...]
    gather x3 -> x0, local copies, waits for them, and re-layouts: 5.46 us -> none  [the longest x1 3.64 us: per_device(): outgoing = table[served]]
  transfers between devices with their start and end apart: 6 -> 0, of which waited for: 6 -> 0; matrix products, arithmetic and copies ran while one was open for 5% -> 0% of each run, Pallas kernels for 0% -> 0%
where the time goes in v1:
time: 116 us
  Pallas kernels  106 us (91%)
  local copies, waits for them, and re-layouts  8.17 us (7%)
  other arithmetic  1.36 us (1%)
    pallas_call x1, Pallas kernels, per_device(): pl.pallas_call(functools.partial(layer_kernel, (n_emb, n_bal, n_rep)), ou...  106 us
    unnamed x14, local copies, waits for them, and re-layouts  7.89 us

profile of v1, /device:TPU:1, one launch (start us, length us, event | category | flops | bytes accessed | tf_op | source)
XLA Modules:
  0.0 116.0 jit_solution(16565512733134711598)
XLA Ops:
  0.6 0.5 broadcast.11
  1.1 1.3 %reduce.3 = s32[512]{0:T(512)S(1)} reduce(s32[1,1,1,512]{3,2,1,0:T(1,128)} %param.8, s32[]{:T(128)} %broadcast.11), dimensions={0,1,2}, to_apply=%param.8.reduce_sub_computation.3 | reduce | bytes 4100 | tf_op args[1]
  2.5 0.1 reshape.22
  2.6 0.1 copy.18
  2.7 0.1 reshape.23.idx_ref
  2.8 0.8 copy.19
  3.6 0.0 copy-start
  3.6 1.6 %copy-done = bf16[512,2048]{1,0:T(8,128)(2,1)S(1)} copy-done((bf16[512,2048]{1,0:T(8,128)(2,1)S(1)}, bf16[512,2048]{1,0:T(8,128)(2,1)}, u32[]{:S(2)}) %copy-start) | copy-done | bytes 2097176
  5.2 0.0 copy-start.1
  5.2 1.0 copy-done.1
  6.2 0.0 copy-start.2
  6.2 0.9 copy-done.2
  7.2 0.0 copy-start.3
  7.2 0.9 copy-done.3
  8.1 0.0 copy-start.4
  8.1 0.7 copy-done.4
  8.7 105.8 %shard_map.86 = (bf16[128,512]{1,0:T(8,128)(2,1)S(1)}, f32[256,512]{1,0:T(8,128)S(1)}) custom-call(bf16[256,512]{1,0:T(8,128)(2,1)S(1)} %copy-done.2, s32[1,1024]{1,0:T(1,128)S(1)} %reshape.23.idx_ref, s32[128,2]{1,0:T(8,128)S(1)} %bitcast.3, s32[1,8]{1,0:T(1,128)S(1)} %copy-done.4, bf16[512,2048]{1,0:T(8,128)(2,1)S(1)} %copy-done, ...), custom_call_target="tpu_custom_call" | custom-call | tf_op jit(solution)/shard_map/pallas_call | solution.py:402
  114.5 0.7 copy.22
  115.2 0.8 copy.23
  (2 shorter events, 0.0 us)
Async XLA Ops:
  3.6 1.6 %copy-start = (bf16[512,2048]{1,0:T(8,128)(2,1)S(1)}, bf16[512,2048]{1,0:T(8,128)(2,1)}, u32[]{:S(2)}) copy-start(bf16[512,2048]{1,0:T(8,128)(2,1)} %w_in_hbm.1) | copy-start | bytes 6291460
  5.2 1.0 copy-start.1
  6.2 0.9 copy-start.2
  7.2 0.9 copy-start.3
  8.1 0.7 copy-start.4

commit v2 on v1

v2 whole, which is shorter than its diff:
```python
import functools
import math

import jax
import jax.numpy as jnp
from jax import lax
from jax.experimental import pallas as pl
from jax.experimental.pallas import tpu as pltpu
from jax.sharding import PartitionSpec as P

HEADS = 4
EPS = 1e-05
MESH = pl.DeviceIdType.MESH
F32 = jnp.float32
BF16 = jnp.bfloat16


def dot(a, b):
    return jnp.dot(a, b, preferred_element_type=F32)


def dot_nt(a, b):
    return lax.dot_general(a, b, (((1,), (1,)), ((), ())), preferred_element_type=F32)


def dot_tn(a, b):
    return lax.dot_general(a, b, (((0,), (0,)), ((), ())), preferred_element_type=F32)


def sigmoid(v):
    return 0.5 * jnp.tanh(0.5 * v) + 0.5


def silu(v):
    return v * sigmoid(v)


def silu_and_slope(v):
    s = sigmoid(v)
    y = v * s
    return y, s + y * (1.0 - s)


def row_mean(v):
    return jnp.mean(v, axis=-1, keepdims=True)


def layer_kernel(
    sizes,
    table_hbm, served_hbm, lookup_hbm, users_ref, w_in_hbm, w_out_hbm, grad_hbm,
    layer_ref, tgrad_ref,
    table, served, lookup, w_in, w_out, grad, zout, zin, zback, zret, onehot, look,
    events, normed, inv_in, act, slope, nrm, datt, kv, qall,
    wt, gt, gq, att, dq, dk, dv, d_mixed, normed_att, dn, gsend, cbuf, hsend, rsbuf, agbuf,
    load_sem, a1_send, a1_recv, x1_send, x1_recv, x2_send, x2_recv,
    a2_send, a2_recv, core_send, core_recv, rs_send, rs_recv, ag_send, ag_recv,
    fan_send, fan_recv,
):
    n_emb, n_bal, n_rep = sizes
    tok, width = grad.shape
    half = width // 2
    slab = zout.shape[0] // n_emb
    cap = slab // 2
    trows = table.shape[0]
    slots = n_emb * cap
    hd = width // HEADS
    inv_root = 1.0 / math.sqrt(hd)
    e = lax.axis_index("emb")
    b = lax.axis_index("bal")
    rep = lax.axis_index("rep")
    share = gsend.shape[0] // n_rep
    part = share // n_bal

    loads = [
        pltpu.make_async_copy(src, dst, load_sem.at[i])
        for i, (src, dst) in enumerate(
            (
                (served_hbm, served), (table_hbm, table), (lookup_hbm, lookup),
                (grad_hbm, grad), (w_out_hbm, w_out), (w_in_hbm, w_in),
            )
        )
    ]
    for load in loads:
        load.start()

    barrier = pltpu.get_barrier_semaphore()

    @pl.loop(1, n_emb)
    def _(k):
        pl.semaphore_signal(
            barrier, inc=1, device_id={"emb": lax.rem(e + k, n_emb)}, device_id_type=MESH
        )

    @pl.loop(1, n_bal)
    def _(k):
        pl.semaphore_signal(
            barrier, inc=1, device_id={"bal": lax.rem(b + k, n_bal)}, device_id_type=MESH
        )

    if n_rep == 2:
        pl.semaphore_signal(barrier, inc=1, device_id={"rep": 1 - rep}, device_id_type=MESH)

    def to_slabs(both):
        halves = [
            both[:, cols].reshape(n_emb, 1, cap, half)
            for cols in (slice(0, half), slice(half, width))
        ]
        return jnp.concatenate(halves, axis=1).reshape(2 * slots, half).astype(BF16)

    def from_slabs(slabs):
        apart = slabs.astype(F32).reshape(n_emb, 2, cap, half)
        return jnp.concatenate(
            [apart[:, h].reshape(slots, half) for h in range(2)], axis=1
        ).astype(BF16)

    loads[0].wait()
    rows_of = lax.broadcasted_iota(jnp.int32, onehot.shape, 0)
    onehot[...] = jnp.where(rows_of == served[...], 1.0, 0.0).astype(BF16)
    loads[1].wait()
    zout[...] = to_slabs(dot_tn(onehot[...], table[...]))

    pl.semaphore_wait(barrier, n_emb + n_bal + n_rep - 3)

    stride = 27 if n_emb % 3 else 1

    def exchange(src, dst, send, recv):
        own = pl.ds(pl.multiple_of(e * slab, slab), slab)

        @pl.loop(1, n_emb)
        def _(k):
            to = lax.rem(e + stride * k, n_emb)
            pltpu.make_async_remote_copy(
                src_ref=src.at[pl.ds(pl.multiple_of(to * slab, slab), slab)],
                dst_ref=dst.at[own],
                send_sem=send,
                recv_sem=recv,
                device_id={"emb": to},
                device_id_type=MESH,
            ).start()

        dst[own, :] = src[own, :]
        many = pl.ds(0, (n_emb - 1) * slab)
        return pltpu.make_async_remote_copy(
            src_ref=src.at[many],
            dst_ref=dst.at[many],
            send_sem=send,
            recv_sem=recv,
            device_id={"emb": lax.rem(e + 1, n_emb)},
            device_id_type=MESH,
        )

    first = exchange(zout, zin, a1_send, a1_recv)

    loads[2].wait()
    slot_of = lax.broadcasted_iota(jnp.int32, look.shape, 0)
    hit = (slot_of == lookup[0:1, :]) | (slot_of == lookup[1:2, :])
    look[...] = jnp.where(hit, 1.0, 0.0).astype(BF16)

    my_user = users_ref[0, b]
    count = jnp.int32(0)
    for k in range(n_bal):
        count = count + jnp.where(users_ref[0, k] == my_user, 1, 0)
    inv_len = jnp.float32(0.0)
    for k in range(1, n_bal + 1):
        inv_len = jnp.where(count == k, jnp.float32(1.0 / (k * tok)), inv_len)

    for load in loads[3:]:
        load.wait()
    d_mixed[...] = dot_nt(grad[...], w_out[...])

    first.wait_recv()
    ev = dot_tn(look[...], from_slabs(zin[...]))
    events[...] = ev
    centered = ev - row_mean(ev)
    inv = lax.rsqrt(row_mean(centered * centered) + EPS)
    inv_in[...] = jnp.broadcast_to(inv, inv_in.shape)
    normed[...] = centered * inv
    nrm[0] = normed[...].astype(BF16)

    rows = tok // 2
    steps = n_bal // 2
    right = lax.rem(b + 1, n_bal)
    left = lax.rem(b + n_bal - 1, n_bal)

    def hop(buf, send, recv, way, step, c):
        if way == 0:
            src, dst, to = lax.rem(n_bal - step, n_bal), n_bal - 1 - step, right
        else:
            src, dst, to = step, step + 1, left
        piece = pl.ds(c * rows, rows)
        return pltpu.make_async_remote_copy(
            src_ref=buf.at[src, piece],
            dst_ref=buf.at[dst, piece],
            send_sem=send.at[way, step, c],
            recv_sem=recv.at[way, step, c],
            device_id={"bal": to},
            device_id_type=MESH,
        )

    lanes = [(way, c) for c in range(2) for way in range(2)]

    def ring_start(buf, send, recv):
        for way, c in lanes:
            if steps > 1 or way == c:
                hop(buf, send, recv, way, 0, c).start()

    def ring_rest(buf, send, recv, own_work, on_block):
        @pl.loop(0, steps + 1)
        def _(step):
            for c in range(2):
                for way in range(2):
                    last = steps - 1 if way == c else steps - 2

                    @pl.when(step <= last)
                    def _():
                        hop(buf, send, recv, way, step, c).wait_recv()

                    @pl.when(step + 1 <= last)
                    def _():
                        hop(buf, send, recv, way, step + 1, c).start()

                @pl.when(step == 0)
                def _():
                    own_work[c]()

            @pl.when(step > 0)
            def _():
                @pl.loop(0, 2)
                def _(k):
                    @pl.when((k == 0) | (step < steps))
                    def _():
                        on_block(jnp.where(k == 0, n_bal - step, step))

    def ring_drain(buf, send, recv):
        @pl.loop(0, steps)
        def _(step):
            for way, c in lanes:
                last = steps - 1 if way == c else steps - 2

                @pl.when(step <= last)
                def _():
                    hop(buf, send, recv, way, step, c).wait_send()

    ring_start(nrm, x1_send, x1_recv)
    v_at, q_at, k_at = width, 2 * width, 3 * width

    def head(h, base=0):
        return slice(base + h * hd, base + (h + 1) * hd)

    def project(*columns):
        for base in columns:
            cols = slice(base, base + width)
            a, s = silu_and_slope(dot(nrm[0], w_in[:, cols]))
            act[:, cols] = a.astype(BF16)
            slope[:, cols] = s

    def own_pair():
        project(0)
        tri_row = lax.broadcasted_iota(jnp.int32, (tok, tok), 0)
        tri_col = lax.broadcasted_iota(jnp.int32, (tok, tok), 1)
        for h in range(HEADS):
            q, k, v = act[:, head(h, q_at)], act[:, head(h, k_at)], act[:, head(h, v_at)]
            y, g = silu_and_slope(dot_nt(q, k) * inv_root)
            keep = tri_row >= tri_col
            att[:, head(h)] = dot(jnp.where(keep, y * inv_len, 0.0).astype(BF16), v)
            gq[0, h] = jnp.where(keep, g * inv_len, 0.0)
            y, g = silu_and_slope(dot_nt(k, q) * inv_root)
            keep = tri_row <= tri_col
            wt[0, h] = jnp.where(keep, y * inv_len, 0.0).astype(BF16)
            gt[0, h] = jnp.where(keep, g * inv_len, 0.0)

    def seen(j):
        return jnp.where(users_ref[0, j] == my_user, inv_len, jnp.float32(0.0))

    def forward_block(r):
        j = lax.rem(b + r, n_bal)
        f = seen(j)

        @pl.when(j < b)
        def _():
            x = nrm[r]
            kv[r, :, :width] = silu(dot(x, w_in[:, v_at : v_at + width])).astype(BF16)
            kv[r, :, width:] = silu(dot(x, w_in[:, k_at : k_at + width])).astype(BF16)
            for h in range(HEADS):
                k = kv[r, :, head(h, width)]
                y, g = silu_and_slope(dot_nt(act[:, head(h, q_at)], k) * inv_root)
                gq[r, h] = g * f
                att[:, head(h)] += dot((y * f).astype(BF16), kv[r, :, head(h)])

        @pl.when(j > b)
        def _():
            qall[r] = silu(dot(nrm[r], w_in[:, q_at : q_at + width])).astype(BF16)
            for h in range(HEADS):
                y, g = silu_and_slope(
                    dot_nt(act[:, head(h, k_at)], qall[r, :, head(h)]) * inv_root
                )
                gt[r, h] = g * f
                wt[r, h] = (y * f).astype(BF16)

    ring_rest(
        nrm, x1_send, x1_recv, (lambda: project(q_at, k_at, v_at), own_pair), forward_block
    )

    at = att[...]
    centered = at - row_mean(at)
    inv_att = lax.rsqrt(row_mean(centered * centered) + EPS)
    na = centered * inv_att
    normed_att[...] = na
    d_gated = d_mixed[...] * act[:, :width].astype(F32)
    d_att = (
        (d_gated - row_mean(d_gated) - na * row_mean(d_gated * na)) * inv_att
    ).astype(BF16)
    datt[0] = d_att
    ring_start(datt, x2_send, x2_recv)

    def own_pair_back():
        for h in range(HEADS):
            q, k, v = act[:, head(h, q_at)], act[:, head(h, k_at)], act[:, head(h, v_at)]
            d = datt[0, :, head(h)]
            ds = (dot_nt(d, v) * gq[0, h]).astype(BF16)
            dq[:, head(h)] = dot(ds, k)
            dv[:, head(h)] = dot(wt[0, h], d)
            dst = (dot_nt(v, d) * gt[0, h]).astype(BF16)
            dk[:, head(h)] = dot(dst, q)

    def layer_and_gate():
        mixed = (normed_att[...] * act[:, :width].astype(F32)).astype(BF16)
        layer_ref[...] = (events[...] + dot(mixed, w_out[...])).astype(BF16)
        d_pre = (d_mixed[...] * normed_att[...] * slope[:, :width]).astype(BF16)
        dn[...] = dot_nt(d_pre, w_in[:, :width])

    def backward_block(r):
        j = lax.rem(b + r, n_bal)

        @pl.when(j < b)
        def _():
            for h in range(HEADS):
                ds = (dot_nt(datt[0, :, head(h)], kv[r, :, head(h)]) * gq[r, h]).astype(BF16)
                dq[:, head(h)] += dot(ds, kv[r, :, head(h, width)])

        @pl.when(j > b)
        def _():
            for h in range(HEADS):
                d = datt[r, :, head(h)]
                dv[:, head(h)] += dot(wt[r, h], d)
                dst = (dot_nt(act[:, head(h, v_at)], d) * gt[r, h]).astype(BF16)
                dk[:, head(h)] += dot(dst, qall[r, :, head(h)])

    ring_rest(datt, x2_send, x2_recv, (own_pair_back, layer_and_gate), backward_block)

    d_normed = dn[...]
    for base, acc, scale in ((v_at, dv, 1.0), (q_at, dq, inv_root), (k_at, dk, inv_root)):
        d_pre = (acc[...] * scale * slope[:, base : base + width]).astype(BF16)
        d_normed = d_normed + dot_nt(d_pre, w_in[:, base : base + width])
    nr = normed[...]
    d_events = (
        grad[...].astype(F32)
        + (d_normed - row_mean(d_normed) - nr * row_mean(d_normed * nr)) * inv_in[:, 0:1]
    ).astype(BF16)

    zback[...] = to_slabs(dot(look[...], d_events))
    second = exchange(zback, zret, a2_send, a2_recv)
    first.wait_send()
    ring_drain(nrm, x1_send, x1_recv)
    ring_drain(datt, x2_send, x2_recv)
    second.wait_recv()
    grads = dot(onehot[...], from_slabs(zret[...])).astype(BF16)
    gsend[:trows, :] = grads[:, :half]
    gsend[trows:, :] = grads[:, half:]

    ours = pl.ds(pl.multiple_of(rep * share, share), share)
    own_part = pl.ds(pl.multiple_of(b * part, part), part)
    if n_rep == 2:
        theirs = pl.ds(pl.multiple_of((1 - rep) * share, share), share)
        swap = pltpu.make_async_remote_copy(
            src_ref=gsend.at[theirs], dst_ref=cbuf, send_sem=core_send, recv_sem=core_recv,
            device_id={"rep": 1 - rep}, device_id_type=MESH,
        )
        swap.start()
        swap.wait_recv()
        hsend[...] = (gsend[ours, :].astype(F32) + cbuf[...].astype(F32)).astype(BF16)
    else:
        hsend[...] = gsend[...]

    @pl.loop(1, n_bal)
    def _(k):
        c = lax.rem(b + k, n_bal)
        pltpu.make_async_remote_copy(
            src_ref=hsend.at[pl.ds(pl.multiple_of(c * part, part), part)],
            dst_ref=rsbuf.at[own_part],
            send_sem=rs_send,
            recv_sem=rs_recv,
            device_id={"bal": c},
            device_id_type=MESH,
        ).start()

    rsbuf[own_part, :] = hsend[own_part, :]
    others = pl.ds(0, (n_bal - 1) * part)
    reduced = pltpu.make_async_remote_copy(
        src_ref=hsend.at[others], dst_ref=rsbuf.at[others],
        send_sem=rs_send, recv_sem=rs_recv, device_id={"bal": right}, device_id_type=MESH,
    )
    second.wait_send()
    reduced.wait_recv()
    total = rsbuf[0:part, :].astype(F32)
    for k in range(1, n_bal):
        total = total + rsbuf[k * part : (k + 1) * part, :].astype(F32)
    mine_at = pl.ds(pl.multiple_of(rep * share + b * part, part), part)
    agbuf[mine_at, :] = total.astype(BF16)

    @pl.loop(1, n_bal)
    def _(k):
        pltpu.make_async_remote_copy(
            src_ref=agbuf.at[mine_at],
            dst_ref=agbuf.at[mine_at],
            send_sem=ag_send,
            recv_sem=ag_recv,
            device_id={"bal": lax.rem(b + k, n_bal)},
            device_id_type=MESH,
        ).start()

    gathered = pltpu.make_async_remote_copy(
        src_ref=agbuf.at[others], dst_ref=agbuf.at[others],
        send_sem=ag_send, recv_sem=ag_recv, device_id={"bal": right}, device_id_type=MESH,
    )
    reduced.wait_send()
    gathered.wait_recv()
    if n_rep == 2:
        fan = pltpu.make_async_remote_copy(
            src_ref=agbuf.at[ours], dst_ref=agbuf.at[ours], send_sem=fan_send,
            recv_sem=fan_recv, device_id={"rep": 1 - rep}, device_id_type=MESH,
        )
        fan.start()
        swap.wait_send()
        fan.wait_recv()
    tgrad_ref[:, :half] = agbuf[:trows, :]
    tgrad_ref[:, half:] = agbuf[trows:, :]
    gathered.wait_send()
    if n_rep == 2:
        fan.wait_send()


def per_device(table, served_rows, w_in, w_out, lookup_slots, block_users, out_grad):
    n_emb, n_bal, n_rep = (lax.axis_size(a) for a in ("emb", "bal", "rep"))
    trows, width = table.shape
    tok = lookup_slots.shape[1]
    half = width // 2
    steps = n_bal // 2
    slots = 2 * served_rows.shape[-1]
    hd = width // HEADS
    vmem = pl.BlockSpec(memory_space=pltpu.VMEM)
    hbm = pl.BlockSpec(memory_space=pltpu.HBM)
    dma = pltpu.SemaphoreType.DMA
    share = 2 * trows // n_rep
    layer_out, table_grad = pl.pallas_call(
        functools.partial(layer_kernel, (n_emb, n_bal, n_rep)),
        out_shape=(
            jax.ShapeDtypeStruct((tok, width), BF16),
            jax.ShapeDtypeStruct((trows, width), BF16),
        ),
        in_specs=[hbm, hbm, hbm, pl.BlockSpec(memory_space=pltpu.SMEM), hbm, hbm, hbm],
        out_specs=(vmem, vmem),
        scratch_shapes=[
            pltpu.VMEM((trows, width), BF16),
            pltpu.VMEM((1, slots // 2), jnp.int32),
            pltpu.VMEM((2, tok), jnp.int32),
            pltpu.VMEM((width, 4 * width), BF16),
            pltpu.VMEM((width, width), BF16),
            pltpu.VMEM((tok, width), BF16),
            pltpu.VMEM((slots, half), BF16),
            pltpu.VMEM((slots, half), BF16),
            pltpu.VMEM((slots, half), BF16),
            pltpu.VMEM((slots, half), BF16),
            pltpu.VMEM((trows, slots // 2), BF16),
            pltpu.VMEM((slots // 2, tok), BF16),
            pltpu.VMEM((tok, width), F32),
            pltpu.VMEM((tok, width), F32),
            pltpu.VMEM((tok, 128), F32),
            pltpu.VMEM((tok, 4 * width), BF16),
            pltpu.VMEM((tok, 4 * width), F32),
            pltpu.VMEM((n_bal, tok, width), BF16),
            pltpu.VMEM((n_bal, tok, width), BF16),
            pltpu.VMEM((n_bal, tok, 2 * width), BF16),
            pltpu.VMEM((n_bal, tok, width), BF16),
            pltpu.VMEM((n_bal, HEADS, tok, tok), BF16),
            pltpu.VMEM((n_bal, HEADS, tok, tok), F32),
            pltpu.VMEM((n_bal, HEADS, tok, tok), F32),
            pltpu.VMEM((tok, width), F32),
            pltpu.VMEM((tok, width), F32),
            pltpu.VMEM((tok, width), F32),
            pltpu.VMEM((tok, width), F32),
            pltpu.VMEM((tok, width), F32),
            pltpu.VMEM((tok, width), F32),
            pltpu.VMEM((tok, width), F32),
            pltpu.VMEM((2 * trows, half), BF16),
            pltpu.VMEM((share, half), BF16),
            pltpu.VMEM((share, half), BF16),
            pltpu.VMEM((share, half), BF16),
            pltpu.VMEM((2 * trows, half), BF16),
            dma((6,)),
            dma, dma,
            dma((2, steps, 2)), dma((2, steps, 2)),
            dma((2, steps, 2)), dma((2, steps, 2)),
            dma, dma, dma, dma, dma, dma, dma, dma, dma, dma,
        ],
        compiler_params=pltpu.CompilerParams(
            collective_id=0, has_side_effects=True, vmem_limit_bytes=56 * 1024 * 1024
        ),
    )(
        table, served_rows.reshape(1, -1), lookup_slots[0].T, block_users, w_in, w_out, out_grad[0],
    )
    return layer_out[None], table_grad.astype(F32)


def solution(mesh):
    placed = (
        P("emb", None),
        P("emb", "bal", "rep", None),
        P(),
        P(),
        P(("emb", "rep"), "bal", None),
        P(("emb", "rep"), None),
        P(("emb", "rep"), "bal", None),
    )
    return jax.shard_map(
        per_device,
        mesh=mesh,
        in_specs=placed,
        out_specs=(P(("emb", "rep"), "bal", None), P("emb", None)),
        check_vma=False,
    )
```

time: 116 us -> 113 us (0.974)
  local copies, waits for them, and re-layouts: 8.17 us -> 1.57 us
  Pallas kernels: 106 us -> 109 us
    unnamed x14 -> x1, local copies, waits for them, and re-layouts: 7.89 us -> 1.57 us
    pallas_call x1, Pallas kernels: 106 us -> 109 us  [per_device(): pl.pallas_call(functools.partial(layer_kernel, (n_emb, n_bal, n_rep)), ou...]
    convert_element_type x0 -> x1, other arithmetic: none -> 1.8 us  [per_device(): return (layer_out[None], table_grad.astype(F32))]
    unnamed x1 -> x0, other arithmetic: 1.34 us -> none
where the time goes in v2:
time: 113 us
  Pallas kernels  109 us (96%)
  other arithmetic  1.8 us (2%)
  local copies, waits for them, and re-layouts  1.57 us (1%)
    pallas_call x1, Pallas kernels, per_device(): pl.pallas_call(functools.partial(layer_kernel, (n_emb, n_bal, n_rep)), ou...  109 us

profile of v2, /device:TPU:1, one launch (start us, length us, event | category | flops | bytes accessed | tf_op | source)
XLA Modules:
  0.0 112.6 jit_solution(10201602609474324596)
XLA Ops:
  0.6 108.6 %shard_map.86 = (bf16[128,512]{1,0:T(8,128)(2,1)}, bf16[256,512]{1,0:T(8,128)(2,1)}) custom-call(bf16[256,512]{1,0:T(8,128)(2,1)} %table_hbm.1, s32[1,512]{1,0:T(1,128)} %bitcast.8, s32[2,128]{1,0:T(2,128)} %bitcast.9, s32[1,8]{1,0:T(1,128)} %users_ref.1, bf16[512,2048]{1,0:T(8,128)(2,1)} %w_in_hbm.1, bf16[512,512]{1,0:T(8,128)(2,1)} %w_out_hbm.1, ...), custom_call_target="tpu_custom_call" | custom-call | tf_op jit(solution)/shard_map/pallas_call | solution.py:455
  109.3 1.8 %convert_element_type.3 = f32[256,512]{1,0:T(8,128)} convert(bf16[256,512]{1,0:T(8,128)(2,1)} %get-tuple-element.5) | non-fusion elementwise | flops 131072 | bytes 786432 | tf_op jit(solution)/shard_map/convert_element_type | solution.py:512
  111.1 1.6 %copy.10 = bf16[1,128,512]{2,1,0:T(8,128)(2,1)} copy(bf16[1,128,512]{2,1,0:T(8,128)(2,1)} %bitcast.6) | data formatting | bytes 262144

commit v3 on v2

--- a/solution.py
+++ b/solution.py
@@ -50,7 +50,7 @@
     table_hbm, served_hbm, lookup_hbm, users_ref, w_in_hbm, w_out_hbm, grad_hbm,
     layer_ref, tgrad_ref,
     table, served, lookup, w_in, w_out, grad, zout, zin, zback, zret, onehot, look,
-    events, normed, inv_in, act, slope, nrm, datt, kv, qall,
+    events, normed, inv_in, act, slope, evs, nrm, datt, kv, qall,
     wt, gt, gq, att, dq, dk, dv, d_mixed, normed_att, dn, gsend, cbuf, hsend, rsbuf, agbuf,
     load_sem, a1_send, a1_recv, x1_send, x1_recv, x2_send, x2_recv,
     a2_send, a2_recv, core_send, core_recv, rs_send, rs_recv, ag_send, ag_recv,
@@ -68,8 +68,9 @@
     e = lax.axis_index("emb")
     b = lax.axis_index("bal")
     rep = lax.axis_index("rep")
-    share = gsend.shape[0] // n_rep
+    share = trows // n_rep
     part = share // n_bal
+    quarter = half // 2
 
     loads = [
         pltpu.make_async_copy(src, dst, load_sem.at[i])
@@ -100,17 +101,26 @@
     if n_rep == 2:
         pl.semaphore_signal(barrier, inc=1, device_id={"rep": 1 - rep}, device_id_type=MESH)
 
-    def to_slabs(both):
-        halves = [
-            both[:, cols].reshape(n_emb, 1, cap, half)
-            for cols in (slice(0, half), slice(half, width))
+    chunks = [pl.ds(c * quarter, quarter) for c in range(2)]
+    wide = [pl.ds(c * half, half) for c in range(2)]
+
+    def to_slabs(rows_f32):
+        copies = [
+            jnp.concatenate(
+                [
+                    rows_f32[:, c * half + h * quarter : c * half + (h + 1) * quarter]
+                    for c in range(2)
+                ],
+                axis=1,
+            ).reshape(n_emb, 1, cap, half)
+            for h in range(2)
         ]
-        return jnp.concatenate(halves, axis=1).reshape(2 * slots, half).astype(BF16)
-
-    def from_slabs(slabs):
-        apart = slabs.astype(F32).reshape(n_emb, 2, cap, half)
+        return jnp.concatenate(copies, axis=1).reshape(2 * slots, half).astype(BF16)
+
+    def from_slabs(chunk):
+        apart = chunk.astype(F32).reshape(n_emb, 2, cap, quarter)
         return jnp.concatenate(
-            [apart[:, h].reshape(slots, half) for h in range(2)], axis=1
+            [apart[:, h].reshape(slots, quarter) for h in range(2)], axis=1
         ).astype(BF16)
 
     loads[0].wait()
@@ -125,29 +135,33 @@
 
     def exchange(src, dst, send, recv):
         own = pl.ds(pl.multiple_of(e * slab, slab), slab)
-
-        @pl.loop(1, n_emb)
-        def _(k):
-            to = lax.rem(e + stride * k, n_emb)
-            pltpu.make_async_remote_copy(
-                src_ref=src.at[pl.ds(pl.multiple_of(to * slab, slab), slab)],
-                dst_ref=dst.at[own],
-                send_sem=send,
-                recv_sem=recv,
-                device_id={"emb": to},
-                device_id_type=MESH,
-            ).start()
-
+        many = pl.ds(0, (n_emb - 1) * slab)
+        waits = []
+        for c in range(2):
+            @pl.loop(1, n_emb)
+            def _(k):
+                to = lax.rem(e + stride * k, n_emb)
+                pltpu.make_async_remote_copy(
+                    src_ref=src.at[pl.ds(pl.multiple_of(to * slab, slab), slab), chunks[c]],
+                    dst_ref=dst.at[own, chunks[c]],
+                    send_sem=send.at[c],
+                    recv_sem=recv.at[c],
+                    device_id={"emb": to},
+                    device_id_type=MESH,
+                ).start()
+
+            waits.append(
+                pltpu.make_async_remote_copy(
+                    src_ref=src.at[many, chunks[c]],
+                    dst_ref=dst.at[many, chunks[c]],
+                    send_sem=send.at[c],
+                    recv_sem=recv.at[c],
+                    device_id={"emb": lax.rem(e + 1, n_emb)},
+                    device_id_type=MESH,
+                )
+            )
         dst[own, :] = src[own, :]
-        many = pl.ds(0, (n_emb - 1) * slab)
-        return pltpu.make_async_remote_copy(
-            src_ref=src.at[many],
-            dst_ref=dst.at[many],
-            send_sem=send,
-            recv_sem=recv,
-            device_id={"emb": lax.rem(e + 1, n_emb)},
-            device_id_type=MESH,
-        )
+        return waits
 
     first = exchange(zout, zin, a1_send, a1_recv)
 
@@ -168,29 +182,21 @@
         load.wait()
     d_mixed[...] = dot_nt(grad[...], w_out[...])
 
-    first.wait_recv()
-    ev = dot_tn(look[...], from_slabs(zin[...]))
-    events[...] = ev
-    centered = ev - row_mean(ev)
-    inv = lax.rsqrt(row_mean(centered * centered) + EPS)
-    inv_in[...] = jnp.broadcast_to(inv, inv_in.shape)
-    normed[...] = centered * inv
-    nrm[0] = normed[...].astype(BF16)
-
     rows = tok // 2
     steps = n_bal // 2
     right = lax.rem(b + 1, n_bal)
     left = lax.rem(b + n_bal - 1, n_bal)
 
-    def hop(buf, send, recv, way, step, c):
+    def hop(ring, way, step, c):
+        buf, lanes_of, send, recv = ring
         if way == 0:
             src, dst, to = lax.rem(n_bal - step, n_bal), n_bal - 1 - step, right
         else:
             src, dst, to = step, step + 1, left
         piece = pl.ds(c * rows, rows)
         return pltpu.make_async_remote_copy(
-            src_ref=buf.at[src, piece],
-            dst_ref=buf.at[dst, piece],
+            src_ref=buf.at[src, piece, lanes_of],
+            dst_ref=buf.at[dst, piece, lanes_of],
             send_sem=send.at[way, step, c],
             recv_sem=recv.at[way, step, c],
             device_id={"bal": to},
@@ -199,13 +205,13 @@
 
     lanes = [(way, c) for c in range(2) for way in range(2)]
 
-    def ring_start(buf, send, recv):
+    def ring_start(ring):
         for way, c in lanes:
             if steps > 1 or way == c:
-                hop(buf, send, recv, way, 0, c).start()
-
-    def ring_rest(buf, send, recv, own_work, on_block):
-        @pl.loop(0, steps + 1)
+                hop(ring, way, 0, c).start()
+
+    def ring_rest(ring, own_work, on_block):
+        @pl.loop(0, steps + 1 if on_block else steps)
         def _(step):
             for c in range(2):
                 for way in range(2):
@@ -213,15 +219,19 @@
 
                     @pl.when(step <= last)
                     def _():
-                        hop(buf, send, recv, way, step, c).wait_recv()
+                        hop(ring, way, step, c).wait_recv()
 
                     @pl.when(step + 1 <= last)
                     def _():
-                        hop(buf, send, recv, way, step + 1, c).start()
-
-                @pl.when(step == 0)
-                def _():
-                    own_work[c]()
+                        hop(ring, way, step + 1, c).start()
+
+                if own_work:
+                    @pl.when(step == 0)
+                    def _():
+                        own_work[c]()
+
+            if on_block is None:
+                return
 
             @pl.when(step > 0)
             def _():
@@ -231,7 +241,7 @@
                     def _():
                         on_block(jnp.where(k == 0, n_bal - step, step))
 
-    def ring_drain(buf, send, recv):
+    def ring_drain(ring):
         @pl.loop(0, steps)
         def _(step):
             for way, c in lanes:
@@ -239,18 +249,43 @@
 
                 @pl.when(step <= last)
                 def _():
-                    hop(buf, send, recv, way, step, c).wait_send()
-
-    ring_start(nrm, x1_send, x1_recv)
+                    hop(ring, way, step, c).wait_send()
+
+    rings = [(evs, wide[c], x1_send.at[c], x1_recv.at[c]) for c in range(2)]
+    whole = (datt, slice(None), x2_send, x2_recv)
+
+    def take_events(c):
+        first[c].wait_recv()
+        ev = dot_tn(look[...], from_slabs(zin[:, chunks[c]]))
+        events[:, wide[c]] = ev
+        evs[0, :, wide[c]] = ev.astype(BF16)
+        ring_start(rings[c])
+
+    take_events(0)
+    ring_rest(rings[0], None, None)
+    take_events(1)
+
+    def normalized(ev):
+        centered = ev - row_mean(ev)
+        inv = lax.rsqrt(row_mean(centered * centered) + EPS)
+        return centered * inv, inv
+
     v_at, q_at, k_at = width, 2 * width, 3 * width
 
     def head(h, base=0):
         return slice(base + h * hd, base + (h + 1) * hd)
+
+    def own_rows():
+        n, inv = normalized(events[...])
+        inv_in[...] = jnp.broadcast_to(inv, inv_in.shape)
+        normed[...] = n
+        nrm[...] = n.astype(BF16)
+        project(q_at, k_at, v_at)
 
     def project(*columns):
         for base in columns:
             cols = slice(base, base + width)
-            a, s = silu_and_slope(dot(nrm[0], w_in[:, cols]))
+            a, s = silu_and_slope(dot(nrm[...], w_in[:, cols]))
             act[:, cols] = a.astype(BF16)
             slope[:, cols] = s
 
@@ -278,7 +313,7 @@
 
         @pl.when(j < b)
         def _():
-            x = nrm[r]
+            x = normalized(evs[r].astype(F32))[0].astype(BF16)
             kv[r, :, :width] = silu(dot(x, w_in[:, v_at : v_at + width])).astype(BF16)
             kv[r, :, width:] = silu(dot(x, w_in[:, k_at : k_at + width])).astype(BF16)
             for h in range(HEADS):
@@ -289,7 +324,8 @@
 
         @pl.when(j > b)
         def _():
-            qall[r] = silu(dot(nrm[r], w_in[:, q_at : q_at + width])).astype(BF16)
+            x = normalized(evs[r].astype(F32))[0].astype(BF16)
+            qall[r] = silu(dot(x, w_in[:, q_at : q_at + width])).astype(BF16)
             for h in range(HEADS):
                 y, g = silu_and_slope(
                     dot_nt(act[:, head(h, k_at)], qall[r, :, head(h)]) * inv_root
@@ -297,21 +333,16 @@
                 gt[r, h] = g * f
                 wt[r, h] = (y * f).astype(BF16)
 
-    ring_rest(
-        nrm, x1_send, x1_recv, (lambda: project(q_at, k_at, v_at), own_pair), forward_block
-    )
-
-    at = att[...]
-    centered = at - row_mean(at)
-    inv_att = lax.rsqrt(row_mean(centered * centered) + EPS)
-    na = centered * inv_att
+    ring_rest(rings[1], (own_rows, own_pair), forward_block)
+
+    na, inv_att = normalized(att[...])
     normed_att[...] = na
     d_gated = d_mixed[...] * act[:, :width].astype(F32)
     d_att = (
         (d_gated - row_mean(d_gated) - na * row_mean(d_gated * na)) * inv_att
     ).astype(BF16)
     datt[0] = d_att
-    ring_start(datt, x2_send, x2_recv)
+    ring_start(whole)
 
     def own_pair_back():
         for h in range(HEADS):
@@ -346,7 +377,7 @@
                 dst = (dot_nt(act[:, head(h, v_at)], d) * gt[r, h]).astype(BF16)
                 dk[:, head(h)] += dot(dst, qall[r, :, head(h)])
 
-    ring_rest(datt, x2_send, x2_recv, (own_pair_back, layer_and_gate), backward_block)
+    ring_rest(whole, (own_pair_back, layer_and_gate), backward_block)
 
     d_normed = dn[...]
     for base, acc, scale in ((v_at, dv, 1.0), (q_at, dq, inv_root), (k_at, dk, inv_root)):
@@ -360,84 +391,91 @@
 
     zback[...] = to_slabs(dot(look[...], d_events))
     second = exchange(zback, zret, a2_send, a2_recv)
-    first.wait_send()
-    ring_drain(nrm, x1_send, x1_recv)
-    ring_drain(datt, x2_send, x2_recv)
-    second.wait_recv()
-    grads = dot(onehot[...], from_slabs(zret[...])).astype(BF16)
-    gsend[:trows, :] = grads[:, :half]
-    gsend[trows:, :] = grads[:, half:]
+    for c in range(2):
+        first[c].wait_send()
+        ring_drain(rings[c])
+    ring_drain(whole)
 
     ours = pl.ds(pl.multiple_of(rep * share, share), share)
+    theirs = pl.ds(pl.multiple_of((n_rep - 1 - rep) * share, share), share)
     own_part = pl.ds(pl.multiple_of(b * part, part), part)
-    if n_rep == 2:
-        theirs = pl.ds(pl.multiple_of((1 - rep) * share, share), share)
-        swap = pltpu.make_async_remote_copy(
-            src_ref=gsend.at[theirs], dst_ref=cbuf, send_sem=core_send, recv_sem=core_recv,
-            device_id={"rep": 1 - rep}, device_id_type=MESH,
-        )
-        swap.start()
-        swap.wait_recv()
-        hsend[...] = (gsend[ours, :].astype(F32) + cbuf[...].astype(F32)).astype(BF16)
-    else:
-        hsend[...] = gsend[...]
-
-    @pl.loop(1, n_bal)
-    def _(k):
-        c = lax.rem(b + k, n_bal)
-        pltpu.make_async_remote_copy(
-            src_ref=hsend.at[pl.ds(pl.multiple_of(c * part, part), part)],
-            dst_ref=rsbuf.at[own_part],
-            send_sem=rs_send,
-            recv_sem=rs_recv,
-            device_id={"bal": c},
-            device_id_type=MESH,
-        ).start()
-
-    rsbuf[own_part, :] = hsend[own_part, :]
+    mine_at = pl.ds(pl.multiple_of(rep * share + b * part, part), part)
     others = pl.ds(0, (n_bal - 1) * part)
-    reduced = pltpu.make_async_remote_copy(
-        src_ref=hsend.at[others], dst_ref=rsbuf.at[others],
-        send_sem=rs_send, recv_sem=rs_recv, device_id={"bal": right}, device_id_type=MESH,
-    )
-    second.wait_send()
-    reduced.wait_recv()
-    total = rsbuf[0:part, :].astype(F32)
-    for k in range(1, n_bal):
-        total = total + rsbuf[k * part : (k + 1) * part, :].astype(F32)
-    mine_at = pl.ds(pl.multiple_of(rep * share + b * part, part), part)
-    agbuf[mine_at, :] = total.astype(BF16)
-
-    @pl.loop(1, n_bal)
-    def _(k):
-        pltpu.make_async_remote_copy(
-            src_ref=agbuf.at[mine_at],
-            dst_ref=agbuf.at[mine_at],
-            send_sem=ag_send,
-            recv_sem=ag_recv,
-            device_id={"bal": lax.rem(b + k, n_bal)},
-            device_id_type=MESH,
-        ).start()
-
-    gathered = pltpu.make_async_remote_copy(
-        src_ref=agbuf.at[others], dst_ref=agbuf.at[others],
-        send_sem=ag_send, recv_sem=ag_recv, device_id={"bal": right}, device_id_type=MESH,
-    )
-    reduced.wait_send()
-    gathered.wait_recv()
-    if n_rep == 2:
-        fan = pltpu.make_async_remote_copy(
-            src_ref=agbuf.at[ours], dst_ref=agbuf.at[ours], send_sem=fan_send,
-            recv_sem=fan_recv, device_id={"rep": 1 - rep}, device_id_type=MESH,
-        )
-        fan.start()
-        swap.wait_send()
-        fan.wait_recv()
-    tgrad_ref[:, :half] = agbuf[:trows, :]
-    tgrad_ref[:, half:] = agbuf[trows:, :]
-    gathered.wait_send()
-    if n_rep == 2:
-        fan.wait_send()
+    other_core = {"rep": n_rep - 1 - rep}
+    pending = []
+
+    def remote(src, dst, send, recv, where):
+        return pltpu.make_async_remote_copy(
+            src_ref=src, dst_ref=dst, send_sem=send, recv_sem=recv,
+            device_id=where, device_id_type=MESH,
+        )
+
+    def reduce_chunk(c):
+        second[c].wait_recv()
+        gsend[c] = dot(onehot[...], from_slabs(zret[:, chunks[c]])).astype(BF16)
+        if n_rep == 2:
+            swap = remote(
+                gsend.at[c, theirs], cbuf.at[c], core_send.at[c], core_recv.at[c], other_core
+            )
+            swap.start()
+            pending.append(swap)
+            swap.wait_recv()
+            hsend[c] = (gsend[c, ours, :].astype(F32) + cbuf[c].astype(F32)).astype(BF16)
+        else:
+            hsend[c] = gsend[c]
+
+        @pl.loop(1, n_bal)
+        def _(k):
+            to = lax.rem(b + k, n_bal)
+            remote(
+                hsend.at[c, pl.ds(pl.multiple_of(to * part, part), part)],
+                rsbuf.at[c, own_part], rs_send.at[c], rs_recv.at[c], {"bal": to},
+            ).start()
+
+        rsbuf[c, own_part, :] = hsend[c, own_part, :]
+        reduced = remote(
+            hsend.at[c, others], rsbuf.at[c, others], rs_send.at[c], rs_recv.at[c],
+            {"bal": right},
+        )
+        pending.append(reduced)
+        reduced.wait_recv()
+        total = rsbuf[c, 0:part, :].astype(F32)
+        for k in range(1, n_bal):
+            total = total + rsbuf[c, k * part : (k + 1) * part, :].astype(F32)
+        agbuf[c, mine_at, :] = total.astype(BF16)
+
+        @pl.loop(1, n_bal)
+        def _(k):
+            remote(
+                agbuf.at[c, mine_at], agbuf.at[c, mine_at], ag_send.at[c], ag_recv.at[c],
+                {"bal": lax.rem(b + k, n_bal)},
+            ).start()
+
+    def finish_chunk(c):
+        gathered = remote(
+            agbuf.at[c, others], agbuf.at[c, others], ag_send.at[c], ag_recv.at[c],
+            {"bal": right},
+        )
+        gathered.wait_recv()
+        pending.append(gathered)
+        if n_rep == 2:
+            fan = remote(
+                agbuf.at[c, ours], agbuf.at[c, ours], fan_send.at[c], fan_recv.at[c], other_core
+            )
+            fan.start()
+            pending.append(fan)
+            return fan
+
+    reduce_chunk(0)
+    fan0 = finish_chunk(0)
+    reduce_chunk(1)
+    fan1 = finish_chunk(1)
+    for c, fan in enumerate((fan0, fan1)):
+        if fan is not None:
+            fan.wait_recv()
+        tgrad_ref[:, wide[c]] = agbuf[c]
+    for copy in second + pending:
+        copy.wait_send()
 
 
 def per_device(table, served_rows, w_in, w_out, lookup_slots, block_users, out_grad):
@@ -451,7 +489,7 @@
     vmem = pl.BlockSpec(memory_space=pltpu.VMEM)
     hbm = pl.BlockSpec(memory_space=pltpu.HBM)
     dma = pltpu.SemaphoreType.DMA
-    share = 2 * trows // n_rep
+    share = trows // n_rep
     layer_out, table_grad = pl.pallas_call(
         functools.partial(layer_kernel, (n_emb, n_bal, n_rep)),
         out_shape=(
@@ -479,6 +517,7 @@
             pltpu.VMEM((tok, 4 * width), BF16),
             pltpu.VMEM((tok, 4 * width), F32),
             pltpu.VMEM((n_bal, tok, width), BF16),
+            pltpu.VMEM((tok, width), BF16),
             pltpu.VMEM((n_bal, tok, width), BF16),
             pltpu.VMEM((n_bal, tok, 2 * width), BF16),
             pltpu.VMEM((n_bal, tok, width), BF16),
@@ -492,16 +531,17 @@
             pltpu.VMEM((tok, width), F32),
             pltpu.VMEM((tok, width), F32),
             pltpu.VMEM((tok, width), F32),
-            pltpu.VMEM((2 * trows, half), BF16),
-            pltpu.VMEM((share, half), BF16),
-            pltpu.VMEM((share, half), BF16),
-            pltpu.VMEM((share, half), BF16),
-            pltpu.VMEM((2 * trows, half), BF16),
+            pltpu.VMEM((2, trows, half), BF16),
+            pltpu.VMEM((2, share, half), BF16),
+            pltpu.VMEM((2, share, half), BF16),
+            pltpu.VMEM((2, share, half), BF16),
+            pltpu.VMEM((2, trows, half), BF16),
             dma((6,)),
-            dma, dma,
+            dma((2,)), dma((2,)),
+            dma((2, 2, steps, 2)), dma((2, 2, steps, 2)),
             dma((2, steps, 2)), dma((2, steps, 2)),
-            dma((2, steps, 2)), dma((2, steps, 2)),
-            dma, dma, dma, dma, dma, dma, dma, dma, dma, dma,
+            dma((2,)), dma((2,)), dma((2,)), dma((2,)), dma((2,)), dma((2,)),
+            dma((2,)), dma((2,)), dma((2,)), dma((2,)),
         ],
         compiler_params=pltpu.CompilerParams(
             collective_id=0, has_side_effects=True, vmem_limit_bytes=56 * 1024 * 1024

time: 113 us -> 126 us (1.12)
  Pallas kernels: 109 us -> 122 us
    pallas_call x1, Pallas kernels: 109 us -> 122 us  [per_device(): pl.pallas_call(functools.partial(layer_kernel, (n_emb, n_bal, n_rep)), ou...]
where the time goes in v3:
time: 126 us
  Pallas kernels  122 us (97%)
  other arithmetic  1.8 us (1%)
  local copies, waits for them, and re-layouts  1.57 us (1%)
    pallas_call x1, Pallas kernels, per_device(): pl.pallas_call(functools.partial(layer_kernel, (n_emb, n_bal, n_rep)), ou...  122 us

profile of v3, /device:TPU:1, one launch (start us, length us, event | category | flops | bytes accessed | tf_op | source)
XLA Modules:
  0.0 126.0 jit_solution(1483250687824015965)
XLA Ops:
  0.6 122.0 %shard_map.86 = (bf16[128,512]{1,0:T(8,128)(2,1)}, bf16[256,512]{1,0:T(8,128)(2,1)}) custom-call(bf16[256,512]{1,0:T(8,128)(2,1)} %table_hbm.1, s32[1,512]{1,0:T(1,128)} %bitcast.8, s32[2,128]{1,0:T(2,128)} %bitcast.9, s32[1,8]{1,0:T(1,128)} %users_ref.1, bf16[512,2048]{1,0:T(8,128)(2,1)} %w_in_hbm.1, bf16[512,512]{1,0:T(8,128)(2,1)} %w_out_hbm.1, ...), custom_call_target="tpu_custom_call" | custom-call | tf_op jit(solution)/shard_map/pallas_call | solution.py:493
  122.7 1.8 %convert_element_type.3 = f32[256,512]{1,0:T(8,128)} convert(bf16[256,512]{1,0:T(8,128)(2,1)} %get-tuple-element.5) | non-fusion elementwise | flops 131072 | bytes 786432 | tf_op jit(solution)/shard_map/convert_element_type | solution.py:552
  124.5 1.6 %copy.10 = bf16[1,128,512]{2,1,0:T(8,128)(2,1)} copy(bf16[1,128,512]{2,1,0:T(8,128)(2,1)} %bitcast.6) | data formatting | bytes 262144

commit v4 on v2

--- a/solution.py
+++ b/solution.py
@@ -177,7 +177,7 @@
     normed[...] = centered * inv
     nrm[0] = normed[...].astype(BF16)
 
-    rows = tok // 2
+    rows = tok // 4
     steps = n_bal // 2
     right = lax.rem(b + 1, n_bal)
     left = lax.rem(b + n_bal - 1, n_bal)
@@ -187,7 +187,7 @@
             src, dst, to = lax.rem(n_bal - step, n_bal), n_bal - 1 - step, right
         else:
             src, dst, to = step, step + 1, left
-        piece = pl.ds(c * rows, rows)
+        piece = pl.ds(pl.multiple_of(c * rows, rows), rows)
         return pltpu.make_async_remote_copy(
             src_ref=buf.at[src, piece],
             dst_ref=buf.at[dst, piece],
@@ -197,55 +197,68 @@
             device_id_type=MESH,
         )
 
-    lanes = [(way, c) for c in range(2) for way in range(2)]
-
-    def ring_start(buf, send, recv):
-        for way, c in lanes:
-            if steps > 1 or way == c:
-                hop(buf, send, recv, way, 0, c).start()
-
-    def ring_rest(buf, send, recv, own_work, on_block):
+    def last_step(way, c):
+        return jnp.where(lax.div(c, 2) == way, steps - 1, steps - 2)
+
+    def used(causal, way, step, origin):
+        if not causal:
+            return step >= 0
+        return origin >= steps if way == 0 else origin > step
+
+    def sent(causal, way, step, c):
+        origin = lax.rem(b + (n_bal - step if way == 0 else step), n_bal)
+        return (step <= last_step(way, c)) & used(causal, way, step, origin)
+
+    def received(causal, way, step, c):
+        origin = lax.rem(b + (n_bal - 1 - step if way == 0 else step + 1), n_bal)
+        return (step <= last_step(way, c)) & used(causal, way, step, origin)
+
+    def ring_start(buf, send, recv, causal):
+        @pl.loop(0, 4)
+        def _(c):
+            for way in range(2):
+                @pl.when(sent(causal, way, 0, c))
+                def _():
+                    hop(buf, send, recv, way, 0, c).start()
+
+    def ring_rest(buf, send, recv, causal, own_head, on_block):
         @pl.loop(0, steps + 1)
         def _(step):
-            for c in range(2):
+            @pl.loop(0, 4)
+            def _(c):
                 for way in range(2):
-                    last = steps - 1 if way == c else steps - 2
-
-                    @pl.when(step <= last)
+                    @pl.when(received(causal, way, step, c))
                     def _():
                         hop(buf, send, recv, way, step, c).wait_recv()
 
-                    @pl.when(step + 1 <= last)
+                    @pl.when(sent(causal, way, step + 1, c))
                     def _():
                         hop(buf, send, recv, way, step + 1, c).start()
 
                 @pl.when(step == 0)
                 def _():
-                    own_work[c]()
-
-            @pl.when(step > 0)
-            def _():
-                @pl.loop(0, 2)
-                def _(k):
-                    @pl.when((k == 0) | (step < steps))
-                    def _():
-                        on_block(jnp.where(k == 0, n_bal - step, step))
-
-    def ring_drain(buf, send, recv):
+                    own_head(c)
+
+                @pl.when((step > 0) & ((c == 1) | ((c == 3) & (step < steps))))
+                def _():
+                    on_block(jnp.where(c == 1, n_bal - step, step))
+
+    def ring_drain(buf, send, recv, causal):
         @pl.loop(0, steps)
         def _(step):
-            for way, c in lanes:
-                last = steps - 1 if way == c else steps - 2
-
-                @pl.when(step <= last)
-                def _():
-                    hop(buf, send, recv, way, step, c).wait_send()
-
-    ring_start(nrm, x1_send, x1_recv)
+            @pl.loop(0, 4)
+            def _(c):
+                for way in range(2):
+                    @pl.when(sent(causal, way, step, c))
+                    def _():
+                        hop(buf, send, recv, way, step, c).wait_send()
+
     v_at, q_at, k_at = width, 2 * width, 3 * width
 
     def head(h, base=0):
-        return slice(base + h * hd, base + (h + 1) * hd)
+        if isinstance(h, int):
+            return slice(base + h * hd, base + (h + 1) * hd)
+        return pl.ds(pl.multiple_of(base + h * hd, hd), hd)
 
     def project(*columns):
         for base in columns:
@@ -254,20 +267,21 @@
             act[:, cols] = a.astype(BF16)
             slope[:, cols] = s
 
-    def own_pair():
-        project(0)
+    def own_pair(h):
         tri_row = lax.broadcasted_iota(jnp.int32, (tok, tok), 0)
         tri_col = lax.broadcasted_iota(jnp.int32, (tok, tok), 1)
-        for h in range(HEADS):
-            q, k, v = act[:, head(h, q_at)], act[:, head(h, k_at)], act[:, head(h, v_at)]
-            y, g = silu_and_slope(dot_nt(q, k) * inv_root)
-            keep = tri_row >= tri_col
-            att[:, head(h)] = dot(jnp.where(keep, y * inv_len, 0.0).astype(BF16), v)
-            gq[0, h] = jnp.where(keep, g * inv_len, 0.0)
-            y, g = silu_and_slope(dot_nt(k, q) * inv_root)
-            keep = tri_row <= tri_col
-            wt[0, h] = jnp.where(keep, y * inv_len, 0.0).astype(BF16)
-            gt[0, h] = jnp.where(keep, g * inv_len, 0.0)
+        q, k, v = act[:, head(h, q_at)], act[:, head(h, k_at)], act[:, head(h, v_at)]
+        y, g = silu_and_slope(dot_nt(q, k) * inv_root)
+        keep = tri_row >= tri_col
+        att[:, head(h)] = dot(jnp.where(keep, y * inv_len, 0.0).astype(BF16), v)
+        gq[0, h] = jnp.where(keep, g * inv_len, 0.0)
+        y, g = silu_and_slope(dot_nt(k, q) * inv_root)
+        keep = tri_row <= tri_col
+        wt[0, h] = jnp.where(keep, y * inv_len, 0.0).astype(BF16)
+        gt[0, h] = jnp.where(keep, g * inv_len, 0.0)
+
+    ring_start(nrm, x1_send, x1_recv, False)
+    project(q_at, k_at, v_at, 0)
 
     def seen(j):
         return jnp.where(users_ref[0, j] == my_user, inv_len, jnp.float32(0.0))
@@ -297,9 +311,7 @@
                 gt[r, h] = g * f
                 wt[r, h] = (y * f).astype(BF16)
 
-    ring_rest(
-        nrm, x1_send, x1_recv, (lambda: project(q_at, k_at, v_at), own_pair), forward_block
-    )
+    ring_rest(nrm, x1_send, x1_recv, False, own_pair, forward_block)
 
     at = att[...]
     centered = at - row_mean(at)
@@ -311,23 +323,27 @@
         (d_gated - row_mean(d_gated) - na * row_mean(d_gated * na)) * inv_att
     ).astype(BF16)
     datt[0] = d_att
-    ring_start(datt, x2_send, x2_recv)
-
-    def own_pair_back():
-        for h in range(HEADS):
-            q, k, v = act[:, head(h, q_at)], act[:, head(h, k_at)], act[:, head(h, v_at)]
-            d = datt[0, :, head(h)]
-            ds = (dot_nt(d, v) * gq[0, h]).astype(BF16)
-            dq[:, head(h)] = dot(ds, k)
-            dv[:, head(h)] = dot(wt[0, h], d)
-            dst = (dot_nt(v, d) * gt[0, h]).astype(BF16)
-            dk[:, head(h)] = dot(dst, q)
-
-    def layer_and_gate():
+
+    def own_pair_back(h):
+        q, k, v = act[:, head(h, q_at)], act[:, head(h, k_at)], act[:, head(h, v_at)]
+        d = datt[0, :, head(h)]
+        ds = (dot_nt(d, v) * gq[0, h]).astype(BF16)
+        dq[:, head(h)] = dot(ds, k)
+        dv[:, head(h)] = dot(wt[0, h], d)
+        dst = (dot_nt(v, d) * gt[0, h]).astype(BF16)
+        dk[:, head(h)] = dot(dst, q)
+
+    def own_layer():
         mixed = (normed_att[...] * act[:, :width].astype(F32)).astype(BF16)
         layer_ref[...] = (events[...] + dot(mixed, w_out[...])).astype(BF16)
+
+    def own_gate():
         d_pre = (d_mixed[...] * normed_att[...] * slope[:, :width]).astype(BF16)
         dn[...] = dot_nt(d_pre, w_in[:, :width])
+
+    ring_start(datt, x2_send, x2_recv, True)
+    own_layer()
+    own_gate()
 
     def backward_block(r):
         j = lax.rem(b + r, n_bal)
@@ -346,7 +362,7 @@
                 dst = (dot_nt(act[:, head(h, v_at)], d) * gt[r, h]).astype(BF16)
                 dk[:, head(h)] += dot(dst, qall[r, :, head(h)])
 
-    ring_rest(datt, x2_send, x2_recv, (own_pair_back, layer_and_gate), backward_block)
+    ring_rest(datt, x2_send, x2_recv, True, own_pair_back, backward_block)
 
     d_normed = dn[...]
     for base, acc, scale in ((v_at, dv, 1.0), (q_at, dq, inv_root), (k_at, dk, inv_root)):
@@ -361,8 +377,8 @@
     zback[...] = to_slabs(dot(look[...], d_events))
     second = exchange(zback, zret, a2_send, a2_recv)
     first.wait_send()
-    ring_drain(nrm, x1_send, x1_recv)
-    ring_drain(datt, x2_send, x2_recv)
+    ring_drain(nrm, x1_send, x1_recv, False)
+    ring_drain(datt, x2_send, x2_recv, True)
     second.wait_recv()
     grads = dot(onehot[...], from_slabs(zret[...])).astype(BF16)
     gsend[:trows, :] = grads[:, :half]
@@ -455,8 +471,8 @@
     layer_out, table_grad = pl.pallas_call(
         functools.partial(layer_kernel, (n_emb, n_bal, n_rep)),
         out_shape=(
-            jax.ShapeDtypeStruct((tok, width), BF16),
-            jax.ShapeDtypeStruct((trows, width), BF16),
+            pltpu.VMEM((tok, width), BF16),
+            pltpu.VMEM((trows, width), BF16),
         ),
         in_specs=[hbm, hbm, hbm, pl.BlockSpec(memory_space=pltpu.SMEM), hbm, hbm, hbm],
         out_specs=(vmem, vmem),
@@ -499,8 +515,8 @@
             pltpu.VMEM((2 * trows, half), BF16),
             dma((6,)),
             dma, dma,
-            dma((2, steps, 2)), dma((2, steps, 2)),
-            dma((2, steps, 2)), dma((2, steps, 2)),
+            dma((2, steps, 4)), dma((2, steps, 4)),
+            dma((2, steps, 4)), dma((2, steps, 4)),
             dma, dma, dma, dma, dma, dma, dma, dma, dma, dma,
         ],
         compiler_params=pltpu.CompilerParams(

time: 113 us -> 107 us (0.947)
  Pallas kernels: 109 us -> 105 us
    pallas_call x1, Pallas kernels: 109 us -> 105 us  [per_device(): pl.pallas_call(functools.partial(layer_kernel, (n_emb, n_bal, n_rep)), ou...]
where the time goes in v4:
time: 107 us
  Pallas kernels  105 us (98%)
    pallas_call x1, Pallas kernels, per_device(): pl.pallas_call(functools.partial(layer_kernel, (n_emb, n_bal, n_rep)), ou...  105 us

profile of v4, /device:TPU:1, one launch (start us, length us, event | category | flops | bytes accessed | tf_op | source)
XLA Modules:
  0.0 107.1 jit_solution(11064558012092360123)
XLA Ops:
  0.6 104.9 %shard_map.86 = (bf16[128,512]{1,0:T(8,128)(2,1)S(1)}, bf16[256,512]{1,0:T(8,128)(2,1)S(1)}) custom-call(bf16[256,512]{1,0:T(8,128)(2,1)} %table_hbm.1, s32[1,512]{1,0:T(1,128)} %bitcast.8, s32[2,128]{1,0:T(2,128)} %bitcast.9, s32[1,8]{1,0:T(1,128)} %users_ref.1, bf16[512,2048]{1,0:T(8,128)(2,1)} %w_in_hbm.1, bf16[512,512]{1,0:T(8,128)(2,1)} %w_out_hbm.1, ...), custom_call_target="tpu_custom_call" | custom-call | tf_op jit(solution)/shard_map/pallas_call | solution.py:471
  105.6 0.7 copy.10
  106.2 0.9 convert_element_type.3

commit v5 on v4

--- a/solution.py
+++ b/solution.py
@@ -68,7 +68,7 @@
     e = lax.axis_index("emb")
     b = lax.axis_index("bal")
     rep = lax.axis_index("rep")
-    share = gsend.shape[0] // n_rep
+    share = trows // n_rep
     part = share // n_bal
 
     loads = [
@@ -380,80 +380,96 @@
     ring_drain(nrm, x1_send, x1_recv, False)
     ring_drain(datt, x2_send, x2_recv, True)
     second.wait_recv()
-    grads = dot(onehot[...], from_slabs(zret[...])).astype(BF16)
-    gsend[:trows, :] = grads[:, :half]
-    gsend[trows:, :] = grads[:, half:]
 
     ours = pl.ds(pl.multiple_of(rep * share, share), share)
+    theirs = pl.ds(pl.multiple_of((n_rep - 1 - rep) * share, share), share)
     own_part = pl.ds(pl.multiple_of(b * part, part), part)
-    if n_rep == 2:
-        theirs = pl.ds(pl.multiple_of((1 - rep) * share, share), share)
-        swap = pltpu.make_async_remote_copy(
-            src_ref=gsend.at[theirs], dst_ref=cbuf, send_sem=core_send, recv_sem=core_recv,
-            device_id={"rep": 1 - rep}, device_id_type=MESH,
-        )
-        swap.start()
-        swap.wait_recv()
-        hsend[...] = (gsend[ours, :].astype(F32) + cbuf[...].astype(F32)).astype(BF16)
-    else:
-        hsend[...] = gsend[...]
-
-    @pl.loop(1, n_bal)
-    def _(k):
-        c = lax.rem(b + k, n_bal)
-        pltpu.make_async_remote_copy(
-            src_ref=hsend.at[pl.ds(pl.multiple_of(c * part, part), part)],
-            dst_ref=rsbuf.at[own_part],
-            send_sem=rs_send,
-            recv_sem=rs_recv,
-            device_id={"bal": c},
-            device_id_type=MESH,
-        ).start()
-
-    rsbuf[own_part, :] = hsend[own_part, :]
+    mine_at = pl.ds(pl.multiple_of(rep * share + b * part, part), part)
     others = pl.ds(0, (n_bal - 1) * part)
-    reduced = pltpu.make_async_remote_copy(
-        src_ref=hsend.at[others], dst_ref=rsbuf.at[others],
-        send_sem=rs_send, recv_sem=rs_recv, device_id={"bal": right}, device_id_type=MESH,
-    )
+    other_core = {"rep": n_rep - 1 - rep}
+
+    def remote(src, dst, send, recv, where):
+        return pltpu.make_async_remote_copy(
+            src_ref=src, dst_ref=dst, send_sem=send, recv_sem=recv,
+            device_id=where, device_id_type=MESH,
+        )
+
+    both = range(2)
+    swaps = [
+        remote(gsend.at[c, theirs], cbuf.at[c], core_send.at[c], core_recv.at[c], other_core)
+        for c in both
+    ]
+    fans = [
+        remote(agbuf.at[c, ours], agbuf.at[c, ours], fan_send.at[c], fan_recv.at[c], other_core)
+        for c in both
+    ]
+    reduced = [
+        remote(
+            hsend.at[c, others], rsbuf.at[c, others], rs_send.at[c], rs_recv.at[c],
+            {"bal": right},
+        )
+        for c in both
+    ]
+    gathered = [
+        remote(
+            agbuf.at[c, others], agbuf.at[c, others], ag_send.at[c], ag_recv.at[c],
+            {"bal": right},
+        )
+        for c in both
+    ]
+    apart = zret[...].astype(F32).reshape(n_emb, 2, cap, half)
+    for c in both:
+        back = apart[:, c].reshape(slots, half).astype(BF16)
+        gsend[c] = dot(onehot[...], back).astype(BF16)
+        if n_rep == 2:
+            swaps[c].start()
+
+    for c in both:
+        if n_rep == 2:
+            swaps[c].wait_recv()
+            hsend[c] = (gsend[c, ours, :].astype(F32) + cbuf[c].astype(F32)).astype(BF16)
+        else:
+            hsend[c] = gsend[c]
+
+        @pl.loop(1, n_bal)
+        def _(k):
+            to = lax.rem(b + k, n_bal)
+            remote(
+                hsend.at[c, pl.ds(pl.multiple_of(to * part, part), part)],
+                rsbuf.at[c, own_part], rs_send.at[c], rs_recv.at[c], {"bal": to},
+            ).start()
+
+        rsbuf[c, own_part, :] = hsend[c, own_part, :]
+
     second.wait_send()
-    reduced.wait_recv()
-    total = rsbuf[0:part, :].astype(F32)
-    for k in range(1, n_bal):
-        total = total + rsbuf[k * part : (k + 1) * part, :].astype(F32)
-    mine_at = pl.ds(pl.multiple_of(rep * share + b * part, part), part)
-    agbuf[mine_at, :] = total.astype(BF16)
-
-    @pl.loop(1, n_bal)
-    def _(k):
-        pltpu.make_async_remote_copy(
-            src_ref=agbuf.at[mine_at],
-            dst_ref=agbuf.at[mine_at],
-            send_sem=ag_send,
-            recv_sem=ag_recv,
-            device_id={"bal": lax.rem(b + k, n_bal)},
-            device_id_type=MESH,
-        ).start()
-
-    gathered = pltpu.make_async_remote_copy(
-        src_ref=agbuf.at[others], dst_ref=agbuf.at[others],
-        send_sem=ag_send, recv_sem=ag_recv, device_id={"bal": right}, device_id_type=MESH,
-    )
-    reduced.wait_send()
-    gathered.wait_recv()
-    if n_rep == 2:
-        fan = pltpu.make_async_remote_copy(
-            src_ref=agbuf.at[ours], dst_ref=agbuf.at[ours], send_sem=fan_send,
-            recv_sem=fan_recv, device_id={"rep": 1 - rep}, device_id_type=MESH,
-        )
-        fan.start()
-        swap.wait_send()
-        fan.wait_recv()
-    tgrad_ref[:, :half] = agbuf[:trows, :]
-    tgrad_ref[:, half:] = agbuf[trows:, :]
-    gathered.wait_send()
-    if n_rep == 2:
-        fan.wait_send()
+    for c in both:
+        reduced[c].wait_recv()
+        total = rsbuf[c, 0:part, :].astype(F32)
+        for k in range(1, n_bal):
+            total = total + rsbuf[c, k * part : (k + 1) * part, :].astype(F32)
+        agbuf[c, mine_at, :] = total.astype(BF16)
+
+        @pl.loop(1, n_bal)
+        def _(k):
+            remote(
+                agbuf.at[c, mine_at], agbuf.at[c, mine_at], ag_send.at[c], ag_recv.at[c],
+                {"bal": lax.rem(b + k, n_bal)},
+            ).start()
+
+    for c in both:
+        gathered[c].wait_recv()
+        if n_rep == 2:
+            fans[c].start()
+    for c in both:
+        if n_rep == 2:
+            fans[c].wait_recv()
+        tgrad_ref[:, c * half : (c + 1) * half] = agbuf[c]
+    for c in both:
+        reduced[c].wait_send()
+        gathered[c].wait_send()
+        if n_rep == 2:
+            swaps[c].wait_send()
+            fans[c].wait_send()
 
 
 def per_device(table, served_rows, w_in, w_out, lookup_slots, block_users, out_grad):
@@ -467,7 +483,7 @@
     vmem = pl.BlockSpec(memory_space=pltpu.VMEM)
     hbm = pl.BlockSpec(memory_space=pltpu.HBM)
     dma = pltpu.SemaphoreType.DMA
-    share = 2 * trows // n_rep
+    share = trows // n_rep
     layer_out, table_grad = pl.pallas_call(
         functools.partial(layer_kernel, (n_emb, n_bal, n_rep)),
         out_shape=(
@@ -508,16 +524,18 @@
             pltpu.VMEM((tok, width), F32),
             pltpu.VMEM((tok, width), F32),
             pltpu.VMEM((tok, width), F32),
-            pltpu.VMEM((2 * trows, half), BF16),
-            pltpu.VMEM((share, half), BF16),
-            pltpu.VMEM((share, half), BF16),
-            pltpu.VMEM((share, half), BF16),
-            pltpu.VMEM((2 * trows, half), BF16),
+            pltpu.VMEM((2, trows, half), BF16),
+            pltpu.VMEM((2, share, half), BF16),
+            pltpu.VMEM((2, share, half), BF16),
+            pltpu.VMEM((2, share, half), BF16),
+            pltpu.VMEM((2, trows, half), BF16),
             dma((6,)),
             dma, dma,
             dma((2, steps, 4)), dma((2, steps, 4)),
             dma((2, steps, 4)), dma((2, steps, 4)),
-            dma, dma, dma, dma, dma, dma, dma, dma, dma, dma,
+            dma, dma,
+            dma((2,)), dma((2,)), dma((2,)), dma((2,)),
+            dma((2,)), dma((2,)), dma((2,)), dma((2,)),
         ],
         compiler_params=pltpu.CompilerParams(
             collective_id=0, has_side_effects=True, vmem_limit_bytes=56 * 1024 * 1024

time: 107 us -> 107 us (level)
  no operation moved by 1% of the time
where the time goes in v5:
time: 107 us; the launch traced here: 106 us
  Pallas kernels  104 us (97%)
    pallas_call x1, Pallas kernels, per_device(): pl.pallas_call(functools.partial(layer_kernel, (n_emb, n_bal, n_rep)), ou...  104 us

profile of v5, /device:TPU:1, one launch (start us, length us, event | category | flops | bytes accessed | tf_op | source)
XLA Modules:
  0.0 106.5 jit_solution(12829274186837378169)
XLA Ops:
  0.6 104.3 %shard_map.86 = (bf16[128,512]{1,0:T(8,128)(2,1)S(1)}, bf16[256,512]{1,0:T(8,128)(2,1)S(1)}) custom-call(bf16[256,512]{1,0:T(8,128)(2,1)} %table_hbm.1, s32[1,512]{1,0:T(1,128)} %bitcast.8, s32[2,128]{1,0:T(2,128)} %bitcast.9, s32[1,8]{1,0:T(1,128)} %users_ref.1, bf16[512,2048]{1,0:T(8,128)(2,1)} %w_in_hbm.1, bf16[512,512]{1,0:T(8,128)(2,1)} %w_out_hbm.1, ...), custom_call_target="tpu_custom_call" | custom-call | tf_op jit(solution)/shard_map/pallas_call | solution.py:487
  104.9 0.7 copy.10
  105.6 0.9 convert_element_type.3

commit v6 on v5

--- a/solution.py
+++ b/solution.py
@@ -126,7 +126,7 @@
     def exchange(src, dst, send, recv):
         own = pl.ds(pl.multiple_of(e * slab, slab), slab)
 
-        @pl.loop(1, n_emb)
+        @pl.loop(1, n_emb, unroll=9 if n_emb % 9 == 1 else 1)
         def _(k):
             to = lax.rem(e + stride * k, n_emb)
             pltpu.make_async_remote_copy(
@@ -431,7 +431,7 @@
         else:
             hsend[c] = gsend[c]
 
-        @pl.loop(1, n_bal)
+        @pl.loop(1, n_bal, unroll=n_bal - 1)
         def _(k):
             to = lax.rem(b + k, n_bal)
             remote(
@@ -449,7 +449,7 @@
             total = total + rsbuf[c, k * part : (k + 1) * part, :].astype(F32)
         agbuf[c, mine_at, :] = total.astype(BF16)
 
-        @pl.loop(1, n_bal)
+        @pl.loop(1, n_bal, unroll=n_bal - 1)
         def _(k):
             remote(
                 agbuf.at[c, mine_at], agbuf.at[c, mine_at], ag_send.at[c], ag_recv.at[c],

time: 107 us -> 107 us (level)
  no operation moved by 1% of the time
where the time goes in v6:
time: 107 us; the launch traced here: 106 us
  Pallas kernels  104 us (97%)
    pallas_call x1, Pallas kernels, per_device(): pl.pallas_call(functools.partial(layer_kernel, (n_emb, n_bal, n_rep)), ou...  104 us

profile of v6, /device:TPU:1, one launch (start us, length us, event | category | flops | bytes accessed | tf_op | source)
XLA Modules:
  0.0 106.5 jit_solution(6990470617997685828)
XLA Ops:
  0.6 104.3 %shard_map.86 = (bf16[128,512]{1,0:T(8,128)(2,1)S(1)}, bf16[256,512]{1,0:T(8,128)(2,1)S(1)}) custom-call(bf16[256,512]{1,0:T(8,128)(2,1)} %table_hbm.1, s32[1,512]{1,0:T(1,128)} %bitcast.8, s32[2,128]{1,0:T(2,128)} %bitcast.9, s32[1,8]{1,0:T(1,128)} %users_ref.1, bf16[512,2048]{1,0:T(8,128)(2,1)} %w_in_hbm.1, bf16[512,512]{1,0:T(8,128)(2,1)} %w_out_hbm.1, ...), custom_call_target="tpu_custom_call" | custom-call | tf_op jit(solution)/shard_map/pallas_call | solution.py:487
  105.0 0.7 copy.10
  105.6 0.9 convert_element_type.3
